TPU v7x, 32 devices: a whole 2x2x4 slice. The times are simulated.
32 devices in a mesh: dp: 2 (over core), fsdp: 4 (over z), tile: 4 (over y, x).
Axes of the slice: x: 2, y: 2, z: 4, core: 2. Of those that a mesh axis runs over, the one named last changes fastest.
Arguments:
- tokens: bfloat16 [8, 8, 128, 1536], P(('dp', 'fsdp'), None, 'tile'), may hold values from -6 to 6
- norm_gain: float32 [1536], replicated, may hold values from 0.25 to 1.75
- query_key_value_weight: bfloat16 [1536, 2304], P('fsdp'), may hold values from -5 to 5
- out_weight: bfloat16 [768, 1536], P('fsdp'), may hold values from -0.21875 to 0.21875
- head_weight: bfloat16 [1536, 320], P('fsdp'), may hold values from -0.15625 to 0.15625
- coarse: float32 [8, 20, 8, 128], P(('dp', 'fsdp'), None, None, 'tile'), may hold values from -36 to 36
- grad_fine: float32 [8, 20, 32, 512], P(('dp', 'fsdp'), None, None, 'tile'), may hold values from -0.6 to 0.6
Outputs:
- fine_grid: float32 [8, 20, 32, 512], P(('dp', 'fsdp'), None, None, 'tile')
- grad_tokens: bfloat16 [8, 8, 128, 1536], P(('dp', 'fsdp'), None, 'tile')
- grad_head: float32 [1536, 320], P('fsdp')
All inputs are finite; a program needn't handle non-finite values.
Results may differ from a plain program's by a relative error of at most 0.0059.
Values may be sent and summed in bfloat16 or wider, within the bound.
A program may use at most 64 MiB of HBM per device.

v0:
```python
import jax
import jax.numpy as jnp
from jax import lax
from jax.sharding import PartitionSpec as P

D = 1536
HEADS = 8
HEAD_DIM = 96
VARS = 20
MARGIN = 8
INNER = 768
HEAD_OUT = 320


EPSILON = 1e-05


def with_halo(shard, sides, width):
    for axis, dim in sides:
        devices, length = (lax.axis_size(axis), shard.shape[dim])
        up = [(i, (i + 1) % devices) for i in range(devices)]
        down = [(j, i) for i, j in up]
        last = lax.slice_in_dim(shard, length - width, length, axis=dim)
        leading = lax.slice_in_dim(shard, 0, width, axis=dim)
        before = lax.ppermute(last, axis, up)
        after = lax.ppermute(leading, axis, down)
        shard = jnp.concatenate([before, shard, after], axis=dim)
    return shard


def from_behind(value, axis, steps):
    count = lax.axis_size(axis)
    pairs = [(source, (source + steps) % count) for source in range(count)]
    return lax.ppermute(value, axis, pairs)


def layer_norm(values):
    average = jnp.mean(values, axis=-1, keepdims=True)
    centred = values - average
    variance = jnp.mean(centred * centred, axis=-1, keepdims=True)
    inverse_dev = lax.rsqrt(variance + EPSILON)
    return (centred * inverse_dev, inverse_dev)


def norm_backward(grad_normed, standard, inverse_dev, norm_gain):
    grad_standard = grad_normed * norm_gain
    first_mean = jnp.mean(grad_standard, axis=-1, keepdims=True)
    second_mean = jnp.mean(grad_standard * standard, axis=-1, keepdims=True)
    return inverse_dev * (grad_standard - first_mean - standard * second_mean)


def attend_forward(queries, keys_values):
    query_count = queries.shape[0]
    key_count = keys_values.shape[0]
    score_scale = HEAD_DIM ** (-0.5)
    query_heads = queries.reshape(query_count, HEADS, HEAD_DIM)
    key_heads = keys_values[:, :INNER].reshape(key_count, HEADS, HEAD_DIM)
    value_heads = keys_values[:, INNER:].reshape(key_count, HEADS, HEAD_DIM)
    scores = (
        jnp.einsum("qhd,khd->hqk", query_heads, key_heads, preferred_element_type=jnp.float32)
        * score_scale
    )
    biggest = jnp.max(scores, axis=-1, keepdims=True)
    exponent = jnp.exp(scores - biggest)
    softmax_out = exponent / jnp.sum(exponent, axis=-1, keepdims=True)
    softmax_low = softmax_out.astype(jnp.bfloat16)
    attended = jnp.einsum(
        "hqk,khd->qhd", softmax_low, value_heads, preferred_element_type=jnp.float32
    )
    return (attended.astype(jnp.bfloat16).reshape(query_count, INNER), softmax_out)


def attend_backward(softmax_out, queries, keys_values, grad_attended):
    query_count = queries.shape[0]
    key_count = keys_values.shape[0]
    score_scale = HEAD_DIM ** (-0.5)
    query_heads = queries.reshape(query_count, HEADS, HEAD_DIM)
    key_heads = keys_values[:, :INNER].reshape(key_count, HEADS, HEAD_DIM)
    value_heads = keys_values[:, INNER:].reshape(key_count, HEADS, HEAD_DIM)
    grad_heads = grad_attended.reshape(query_count, HEADS, HEAD_DIM)
    softmax_low = softmax_out.astype(jnp.bfloat16)
    grad_values = jnp.einsum(
        "hqk,qhd->khd", softmax_low, grad_heads, preferred_element_type=jnp.float32
    )
    grad_weights = jnp.einsum(
        "qhd,khd->hqk", grad_heads, value_heads, preferred_element_type=jnp.float32
    )
    weighted = jnp.sum(softmax_out * grad_weights, axis=-1, keepdims=True)
    grad_scores = (softmax_out * (grad_weights - weighted)).astype(jnp.bfloat16)
    grad_queries = (
        jnp.einsum("hqk,khd->qhd", grad_scores, key_heads, preferred_element_type=jnp.float32)
        * score_scale
    )
    grad_keys = (
        jnp.einsum("hqk,qhd->khd", grad_scores, query_heads, preferred_element_type=jnp.float32)
        * score_scale
    )
    pair_gradient_rows = jnp.concatenate(
        [grad_keys.reshape(key_count, INNER), grad_values.reshape(key_count, INNER)], axis=1
    )
    return (grad_queries.astype(jnp.bfloat16).reshape(query_count, INNER), pair_gradient_rows)


def interp_weights(fine_index):
    coarse_cell = fine_index // 4
    phase_index = fine_index % 4
    lower_shift = (phase_index < 2).astype(jnp.int32)
    upper_weight = (2 * phase_index - 3 + 8 * lower_shift).astype(jnp.float32) / 8.0
    return (coarse_cell - lower_shift, upper_weight)


def build_matrix(lower_cell, upper_cell, upper_weight, count):
    columns = jnp.arange(count, dtype=jnp.int32)
    lower_part = jnp.where(
        columns[None, :] == lower_cell[:, None], 1.0 - upper_weight[:, None], 0.0
    )
    upper_portion = jnp.where(columns[None, :] == upper_cell[:, None], upper_weight[:, None], 0.0)
    return lower_part + upper_portion


def contract_last(left_side, right_side):
    return lax.dot_general(
        left_side, right_side, (((1,), (1,)), ((), ())), preferred_element_type=jnp.float32
    )


def shards(tokens, norm_gain, query_key_value_weight, out_weight, head_weight, coarse, grad_fine):
    lat_rows = tokens.shape[1]
    lon_cols = tokens.shape[2]
    row_count = lat_rows * lon_cols
    flattened_rows = tokens[0].reshape(row_count, D).astype(jnp.float32)
    standard, inverse_dev = layer_norm(flattened_rows)
    normed = (standard * norm_gain).astype(jnp.bfloat16)
    full_qkv = lax.all_gather(query_key_value_weight, "fsdp", axis=0, tiled=True)
    projected = jnp.dot(normed, full_qkv, preferred_element_type=jnp.float32).astype(jnp.bfloat16)
    queries = projected[:, :INNER]
    pairs_local = projected[:, INNER:]
    margin_pairs = with_halo(
        pairs_local.reshape(lat_rows, lon_cols, 2 * INNER), (("tile", 1),), MARGIN
    )
    keys_values = margin_pairs.reshape(lat_rows * (lon_cols + 2 * MARGIN), 2 * INNER)
    attended, softmax_out = attend_forward(queries, keys_values)
    full_out = lax.all_gather(out_weight, "fsdp", axis=0, tiled=True)
    mixed_out = jnp.dot(attended, full_out, preferred_element_type=jnp.float32)
    hidden = (flattened_rows + mixed_out).astype(jnp.bfloat16)
    full_head = lax.all_gather(head_weight, "fsdp", axis=0, tiled=True)
    head_out = jnp.dot(hidden, full_head, preferred_element_type=jnp.float32)
    fine_head = (
        head_out.reshape(lat_rows, lon_cols, VARS, 4, 4)
        .transpose(2, 0, 3, 1, 4)
        .reshape(VARS, 4 * lat_rows, 4 * lon_cols)
    )
    coarse_padded_grid = with_halo(coarse[0], (("tile", 2),), 1)
    lat_lower, lat_upper_weight = interp_weights(jnp.arange(4 * lat_rows, dtype=jnp.int32))
    latitude_matrix = build_matrix(
        jnp.clip(lat_lower, 0, lat_rows - 1),
        jnp.clip(lat_lower + 1, 0, lat_rows - 1),
        lat_upper_weight,
        lat_rows,
    )
    lon_lower, lon_upper_weight = interp_weights(jnp.arange(4 * lon_cols, dtype=jnp.int32))
    lon_matrix = build_matrix(lon_lower + 1, lon_lower + 2, lon_upper_weight, lon_cols + 2)
    incomplete_grid = jnp.einsum(
        "lj,kji->kli", latitude_matrix, coarse_padded_grid, precision=lax.Precision.HIGHEST
    )
    residual = jnp.einsum(
        "vrb,cb->vrc", incomplete_grid, lon_matrix, precision=lax.Precision.HIGHEST
    )
    fine_grid = fine_head + residual
    grad_rows = (
        grad_fine[0]
        .reshape(VARS, lat_rows, 4, lon_cols, 4)
        .transpose(1, 3, 0, 2, 4)
        .reshape(row_count, HEAD_OUT)
    )
    grad_rows = grad_rows.astype(jnp.bfloat16)
    head_term = lax.dot_general(
        hidden, grad_rows, (((0,), (0,)), ((), ())), preferred_element_type=jnp.float32
    )
    head_block = lax.psum_scatter(head_term, "fsdp", scatter_dimension=0, tiled=True)
    grad_head = lax.psum(head_block, ("dp", "tile"))
    grad_hidden = contract_last(grad_rows, full_head)
    grad_attended = contract_last(grad_hidden.astype(jnp.bfloat16), full_out).astype(jnp.bfloat16)
    grad_queries, pair_gradient_rows = attend_backward(
        softmax_out, queries, keys_values, grad_attended
    )
    pair_gradient_rows = pair_gradient_rows.reshape(lat_rows, lon_cols + 2 * MARGIN, 2 * INNER)
    from_left = from_behind(pair_gradient_rows[:, lon_cols + MARGIN :], "tile", 1)
    from_right = from_behind(pair_gradient_rows[:, :MARGIN], "tile", -1)
    own_cells = pair_gradient_rows[:, MARGIN : MARGIN + lon_cols]
    own_cells = own_cells + jnp.pad(from_left, ((0, 0), (0, lon_cols - MARGIN), (0, 0)))
    own_cells = own_cells + jnp.pad(from_right, ((0, 0), (lon_cols - MARGIN, 0), (0, 0)))
    grad_all = jnp.concatenate(
        [grad_queries, own_cells.reshape(row_count, 2 * INNER).astype(jnp.bfloat16)], axis=1
    )
    grad_normed = contract_last(grad_all, full_qkv)
    grad_input = grad_hidden + norm_backward(grad_normed, standard, inverse_dev, norm_gain)
    grad_tokens = grad_input.astype(jnp.bfloat16).reshape(1, lat_rows, lon_cols, D)
    return (fine_grid[None], grad_tokens, grad_head)


def solution(mesh):
    placed = (
        P(("dp", "fsdp"), None, "tile", None),
        P(),
        P("fsdp", None),
        P("fsdp", None),
        P("fsdp", None),
        P(("dp", "fsdp"), None, None, "tile"),
        P(("dp", "fsdp"), None, None, "tile"),
    )
    return jax.shard_map(
        shards,
        mesh=mesh,
        in_specs=placed,
        out_specs=(
            P(("dp", "fsdp"), None, None, "tile"),
            P(("dp", "fsdp"), None, "tile", None),
            P("fsdp", None),
        ),
        check_vma=False,
    )
```

profile of v0, /device:TPU:0, one launch (start us, length us, event | category | flops | bytes accessed | tf_op | source)
XLA Modules:
  0.0 352.5 jit_solution(1726271325023431040)
XLA Ops:
  8.8 3.9 %collective-permute-start.3 = (f32[20,8,1]{2,1,0:T(8,128)}, f32[20,8,1]{2,1,0:T(8,128)}, u32[]{:S(2)}, u32[]{:S(2)}) collective-permute-start(f32[20,8,1]{2,1,0:T(8,128)} %get-tuple-element.12), channel_id=1, source_target_pairs={{1,0},{2,1},{3,2},{0,3},{5,4},{6,5},{7,6},{4,7},{9,8},{10,9},{11,1... | collective-permute-start | bytes 1928 | tf_op jit(solution)/shard_map/ppermute | solution.py:26
  16.6 35.7 %all_gather.11 = bf16[1536,320]{0,1:T(8,128)(2,1)S(1)} all-gather(bf16[384,320]{0,1:T(8,128)(2,1)} %param.11), channel_id=1, replica_groups=mesh['dp'=2,'fsdp'=4,'tile'=4] {'fsdp'}, dimensions={0}, use_global_device_ids=true | all-gather | bytes 1228800 | tf_op jit(solution)/shard_map/all_gather | solution.py:146
  54.8 2.1 convolution_bitcast_fusion.1
  56.9 95.1 %all-gather.3.cloned.1.call-done = bf16[1536,2304]{1,0:T(8,128)(2,1)} async-done(((bf16[384,2304]{1,0:T(8,128)(2,1)}), bf16[1536,2304]{1,0:T(8,128)(2,1)}) %all-gather.3.cloned.1.call-update) | async-done | bytes 7077904 | tf_op jit(solution)/shard_map/all_gather | solution.py:134
  152.0 5.3 %convolution_convert_fusion = bf16[256,2304]{1,0:T(8,128)(2,1)S(1)} fusion(bf16[256,1536]{1,0:T(8,128)(2,1)} %multiply_convert_fusion.1, bf16[1536,2304]{1,0:T(8,128)(2,1)} %all-gather.3.cloned.1.call-done), kind=kOutput, calls=%fused_computation.1 | convolution fusion | flops 1812529152 | bytes 9043968 | tf_op jit(solution)/shard_map/dot_general | solution.py:135
  159.1 2.6 collective-permute-start.1
  161.7 41.8 %all-gather.5.cloned.1.call-done = bf16[768,1536]{1,0:T(8,128)(2,1)} async-done(((bf16[192,1536]{1,0:T(8,128)(2,1)}), bf16[768,1536]{1,0:T(8,128)(2,1)}) %all-gather.5.cloned.1.call-update) | async-done | bytes 2359312 | tf_op jit(solution)/shard_map/all_gather | solution.py:143
  203.4 3.2 convolution_convert_fusion.1
  206.7 1.9 copy.24
  208.6 1.8 slice.50
  210.4 1.9 copy.18
  214.8 2.1 copy.28
  216.9 2.2 copy.29
  219.0 4.0 %fusion.57 = (f32[8,256]{1,0:T(8,128)S(1)}, f32[8,256,384]{2,1,0:T(8,128)}) fusion(bf16[256,8,96]{0,2,1:T(8,128)(2,1)} %bitcast.85, bf16[384,8,96]{0,2,1:T(8,128)(2,1)} %bitcast.79), kind=kOutput, calls=%fused_computation.109 | convolution fusion | flops 153354624 | bytes 4136960 | tf_op jit(solution)/shard_map/sub | solution.py:64
  223.1 2.9 convolution_convert_fusion.2
  228.0 1.8 fusion.60
  231.2 3.1 copy.20
  234.3 3.1 copy.21
  237.4 4.4 %multiply_reduce_fusion = (f32[8,256]{1,0:T(8,128)S(1)}, f32[8,256,384]{2,1,0:T(8,128)}) fusion(f32[8,256,384]{2,1,0:T(8,128)} %get-tuple-element.14, f32[8,256]{1,0:T(8,128)S(1)} %get-tuple-element.13, bf16[256,8,96]{0,2,1:T(8,128)(2,1)S(1)} %bitcast.96, bf16[384,8,96]{0,2,1:T(8,128)(2,1)S(1)} %bitcast.93), kind=kOutput, calls=%fused_computation.3 | convolution fusion | flops 153352192 | bytes 7290880 | tf_op jit(solution)/shard_map/qhd,khd->hqk/dot_general | solution.py:85
  242.0 3.3 multiply_convert_fusion
  248.5 1.9 concatenate.19
  250.4 3.6 %convolution_bitcast_fusion = f32[384,8,96]{0,2,1:T(8,128)} fusion(bf16[256,8,96]{0,2,1:T(8,128)(2,1)} %bitcast.95, f32[8,256,384]{2,1,0:T(8,128)} %get-tuple-element.14, f32[8,256]{1,0:T(8,128)S(1)} %get-tuple-element.13), kind=kOutput, calls=%fused_computation.21 | convolution fusion | flops 152567808 | bytes 4726784 | tf_op jit(solution)/shard_map/hqk,qhd->khd/dot_general | solution.py:82
  254.0 2.9 copy.26
  256.9 2.8 concatenate.20
  263.5 2.4 collective-permute-start.5
  268.7 7.1 %collective-permute-done.5 = f32[8,8,1536]{2,1,0:T(8,128)} collective-permute-done((f32[8,8,1536]{2,1,0:T(8,128)}, f32[8,8,1536]{2,1,0:T(8,128)}, u32[]{:S(2)}, u32[]{:S(2)}) %collective-permute-start.5) | collective-permute-done | bytes 393248 | tf_op jit(solution)/shard_map/ppermute | solution.py:34
  275.8 8.1 %collective-permute-done.4 = f32[8,8,1536]{2,1,0:T(8,128)} collective-permute-done((f32[8,8,1536]{2,1,0:T(8,128)}, f32[8,8,1536]{2,1,0:T(8,128)}, u32[]{:S(2)}, u32[]{:S(2)}) %collective-permute-start.4) | collective-permute-done | bytes 393248 | tf_op jit(solution)/shard_map/ppermute | solution.py:34
  283.9 1.7 fusion.6
  285.7 6.2 %fusion.52 = (f32[256]{0:T(256)S(1)}, f32[256]{0:T(256)S(1)}, f32[256,1536]{1,0:T(8,128)}) fusion(f32[256]{0:T(256)S(1)} %rsqrt.12, f32[256]{0:T(256)S(1)} %div.51, bf16[1,8,32,1536]{3,2,1,0:T(8,128)(2,1)S(1)} %copy-done, f32[1536]{0:T(1024)S(1)} %copy-done.20, bf16[1536,2304]{1,0:T(8,128)(2,1)} %all-gather.3.cloned.1.call-done, ...), kind=kOutput, calls=%fused_computation.104 | convolution fusion | flops 1817050624 | bytes 10627072 | tf_op jit(solution)/shard_map/dot_general | solution.py:122
  291.9 2.9 add_convert_fusion
  294.8 49.3 %all-reduce.4.cloned.1.call-done = f32[384,320]{0,1:T(8,128)} async-done(((f32[384,320]{0,1:T(8,128)}), f32[384,320]{0,1:T(8,128)}) %all-reduce.4.cloned.1.call-update) | async-done | bytes 491536 | tf_op jit(solution)/shard_map/psum | solution.py:181
  344.1 1.8 copy.32
  (99 shorter events, 25.6 us)
Async XLA Ops:
  7.2 5.6 %copy-start = (bf16[1,8,32,1536]{3,2,1,0:T(8,128)(2,1)S(1)}, bf16[1,8,32,1536]{3,2,1,0:T(8,128)(2,1)}, u32[]{:S(2)}) copy-start(bf16[1,8,32,1536]{3,2,1,0:T(8,128)(2,1)} %param.7) | copy-start | bytes 2359300
  7.2 144.8 %all-gather.3.cloned.1.call-start = ((), (), s32[]{:S(2)}) async-start(), calls=%async_computation.1 | async-start | bytes 8847360 | tf_op jit(solution)/shard_map/all_gather | solution.py:134
  7.9 5.6 %copy-start.18 = (f32[1,20,32,128]{3,2,1,0:T(8,128)S(1)}, f32[1,20,32,128]{3,2,1,0:T(8,128)}, u32[]{:S(2)}) copy-start(f32[1,20,32,128]{3,2,1,0:T(8,128)} %param.13) | copy-start | bytes 983044
  7.9 195.5 %all-gather.5.cloned.1.call-start = ((), (), s32[]{:S(2)}) async-start(), calls=%async_computation.2 | async-start | bytes 2949120 | tf_op jit(solution)/shard_map/all_gather | solution.py:143
  8.8 46.0 %collective-permute-start.3 = (f32[20,8,1]{2,1,0:T(8,128)}, f32[20,8,1]{2,1,0:T(8,128)}, u32[]{:S(2)}, u32[]{:S(2)}) collective-permute-start(f32[20,8,1]{2,1,0:T(8,128)} %get-tuple-element.12), channel_id=1, source_target_pairs={{1,0},{2,1},{3,2},{0,3},{5,4},{6,5},{7,6},{4,7},{9,8},{10,9},{11,1... | collective-permute-start | bytes 1928 | tf_op jit(solution)/shard_map/ppermute | solution.py:26
  12.7 42.1 %collective-permute-start.2 = (f32[20,8,1]{2,1,0:T(8,128)}, f32[20,8,1]{2,1,0:T(8,128)}, u32[]{:S(2)}, u32[]{:S(2)}) collective-permute-start(f32[20,8,1]{2,1,0:T(8,128)} %get-tuple-element.11), channel_id=1, source_target_pairs={{0,1},{1,2},{2,3},{3,0},{4,5},{5,6},{6,7},{7,4},{8,9},{9,10},{10,1... | collective-permute-start | bytes 1928 | tf_op jit(solution)/shard_map/ppermute | solution.py:25
  12.7 279.2 %reduce-scatter.2.cloned.1.call-start = ((), (), s32[]{:S(2)}) async-start(), calls=%async_computation.3 | async-start | bytes 2457600 | tf_op jit(solution)/shard_map/reduce_scatter | solution.py:180
  52.3 2.5 copy-start.14
  157.2 1.8 copy-start.12
  159.1 53.2 %collective-permute-start.1 = (bf16[8,8,1536]{2,1,0:T(8,128)(2,1)}, bf16[8,8,1536]{2,1,0:T(8,128)(2,1)}, u32[]{:S(2)}, u32[]{:S(2)}) collective-permute-start(bf16[8,8,1536]{2,1,0:T(8,128)(2,1)} %get-tuple-element.10), channel_id=1, source_target_pairs={{1,0},{2,1},{3,2},{0,3},{5,4},{6,5},{7,6},{4,7},{9,8},{10,9},{11,1... | collective-permute-start | bytes 589832 | tf_op jit(solution)/shard_map/ppermute | solution.py:26
  161.7 50.6 %collective-permute-start = (bf16[8,8,1536]{2,1,0:T(8,128)(2,1)}, bf16[8,8,1536]{2,1,0:T(8,128)(2,1)}, u32[]{:S(2)}, u32[]{:S(2)}) collective-permute-start(bf16[8,8,1536]{2,1,0:T(8,128)(2,1)} %get-tuple-element.9), channel_id=1, source_target_pairs={{0,1},{1,2},{2,3},{3,0},{4,5},{5,6},{6,7},{7,4},{8,9},{9,10},{10,1... | collective-permute-start | bytes 589832 | tf_op jit(solution)/shard_map/ppermute | solution.py:25
  223.1 2.9 copy-start.3
  228.0 1.8 copy-start.11
  234.3 3.1 copy-start.15
  234.3 3.1 copy-start.16
  241.8 102.4 %all-reduce.4.cloned.1.call-start = ((), (), s32[]{:S(2)}) async-start(), calls=%async_computation.4 | async-start | bytes 983040 | tf_op jit(solution)/shard_map/psum | solution.py:181
  242.0 4.5 %copy-start.8 = (bf16[256,768]{0,1:T(8,128)(2,1)S(1)}, bf16[256,768]{0,1:T(8,128)(2,1)}, u32[]{:S(2)}) copy-start(bf16[256,768]{0,1:T(8,128)(2,1)} %copy.18) | copy-start | bytes 1179652
  245.3 1.2 copy-start.1
  259.6 1.3 copy-start.7
  260.9 5.0 %copy-start.2 = (bf16[8,256,384]{2,1,0:T(8,128)(2,1)S(1)}, bf16[8,256,384]{2,1,0:T(8,128)(2,1)}, u32[]{:S(2)}) copy-start(bf16[8,256,384]{2,1,0:T(8,128)(2,1)} %copy-done.1) | copy-start | bytes 4718596
  260.9 5.0 %copy-start.5 = (bf16[384,768]{0,1:T(8,128)(2,1)S(1)}, bf16[384,768]{0,1:T(8,128)(2,1)}, u32[]{:S(2)}) copy-start(bf16[384,768]{0,1:T(8,128)(2,1)} %copy.29) | copy-start | bytes 1769476
  261.1 1.5 copy-start.4
  263.5 12.3 %collective-permute-start.5 = (f32[8,8,1536]{2,1,0:T(8,128)}, f32[8,8,1536]{2,1,0:T(8,128)}, u32[]{:S(2)}, u32[]{:S(2)}) collective-permute-start(f32[8,8,1536]{2,1,0:T(8,128)} %get-tuple-element.6), channel_id=1, source_target_pairs={{0,3},{1,0},{2,1},{3,2},{4,7},{5,4},{6,5},{7,6},{8,11},{9,8},{10,9... | collective-permute-start | bytes 1179656 | tf_op jit(solution)/shard_map/ppermute | solution.py:34
  265.8 1.7 copy-start.9
  265.9 1.7 copy-start.10
  265.9 1.7 copy-start.21
  265.9 1.7 copy-start.22
  265.9 1.7 copy-start.23
  265.9 1.7 copy-start.24
  265.9 18.1 %collective-permute-start.4 = (f32[8,8,1536]{2,1,0:T(8,128)}, f32[8,8,1536]{2,1,0:T(8,128)}, u32[]{:S(2)}, u32[]{:S(2)}) collective-permute-start(f32[8,8,1536]{2,1,0:T(8,128)} %get-tuple-element.5), channel_id=1, source_target_pairs={{0,1},{1,2},{2,3},{3,0},{4,5},{5,6},{6,7},{7,4},{8,9},{9,10},{10,1... | collective-permute-start | bytes 1179656 | tf_op jit(solution)/shard_map/ppermute | solution.py:34
  268.7 16.9 %copy-start.17 = (bf16[256,768]{1,0:T(8,128)(2,1)S(1)}, bf16[256,768]{1,0:T(8,128)(2,1)}, u32[]{:S(2)}) copy-start(bf16[256,768]{1,0:T(8,128)(2,1)} %copy.27) | copy-start | bytes 1179652
  268.7 17.0 %copy-start.20 = (f32[1536]{0:T(1024)S(1)}, f32[1536]{0:T(1024)}, u32[]{:S(2)}) copy-start(f32[1536]{0:T(1024)} %param.8) | copy-start | bytes 18436
  (3 other events, 2.5 us)
Sparse Core Ops, SparseCore 0:
  9.6 142.3 all-gather.2
  153.5 49.8 all-gather.4
  241.9 40.2 reduce-scatter.1
  292.1 52.0 all-reduce.3
where the time goes:
time: 353 us
  waiting for transfers between devices  202 us (57%)
  local copies, waits for them, and re-layouts  40.8 us (12%)
  matrix products  38.3 us (11%)
  blocking collectives  35.7 us (10%)
  between operations  14.1 us (4%)
  other arithmetic  12.1 us (3%)
  starting transfers between devices  9.31 us (3%)
    all_gather x1, waiting for transfers between devices, shards(): lax.all_gather(query_key_value_weight, 'fsdp', axis=0, tiled=True)  95.1 us
    psum x1, waiting for transfers between devices, shards(): grad_head = lax.psum(head_block, ('dp', 'tile'))  49.3 us
    all_gather x1, waiting for transfers between devices, shards(): full_out = lax.all_gather(out_weight, 'fsdp', axis=0, tiled=True)  41.8 us
    all_gather x1, blocking collectives, shards(): full_head = lax.all_gather(head_weight, 'fsdp', axis=0, tiled=True)  35.7 us
    ppermute x2, waiting for transfers between devices, from_behind(): return lax.ppermute(value, axis, pairs)  15.2 us
    unnamed x54, local copies, waits for them, and re-layouts  11.2 us
    dot_general x3, matrix products, contract_last(): lax.dot_general(left_side, right_side, (((1,), (1,)), ((), ())), preferre...  10 us
  transfers between devices with their start and end apart: 10, of which 5 were waited for; matrix products, arithmetic and copies ran while one was open for 16% of the time, Pallas kernels for 0%

commit v1 on v0

--- a/solution.py
+++ b/solution.py
@@ -1,6 +1,10 @@
+import functools
+
 import jax
 import jax.numpy as jnp
 from jax import lax
+from jax.experimental import pallas as pl
+from jax.experimental.pallas import tpu as pltpu
 from jax.sharding import PartitionSpec as P
 
 D = 1536
@@ -122,6 +126,646 @@
     return lax.dot_general(
         left_side, right_side, (((1,), (1,)), ((), ())), preferred_element_type=jnp.float32
     )
+
+
+def dot_nt(left_side, right_side):
+    return lax.dot_general(
+        left_side, right_side, (((1,), (1,)), ((), ())), preferred_element_type=jnp.float32
+    )
+
+
+def dot_tn(left_side, right_side):
+    return lax.dot_general(
+        left_side, right_side, (((0,), (0,)), ((), ())), preferred_element_type=jnp.float32
+    )
+
+
+def dot_nn(left_side, right_side):
+    return jnp.dot(left_side, right_side, preferred_element_type=jnp.float32)
+
+
+HEAD, OUT0, OUT1, KEY, VALUE, QUERY0, QUERY1 = range(7)
+ROUTES = (0, 0, 1, 0, 1, 0, 1)
+HALF = INNER // 2
+GROUP = 4
+GROUP_WIDTH = GROUP * HEAD_DIM
+
+
+def block_kernel(
+    fsdp,
+    lat_rows,
+    lon_cols,
+    tokens_ref,
+    gain_ref,
+    qkv_ref,
+    out_ref,
+    head_ref,
+    grad_rows_ref,
+    head_out_ref,
+    grad_tokens_ref,
+    grad_head_ref,
+    w_head,
+    w_out0,
+    w_out1,
+    w_key,
+    w_value,
+    w_query0,
+    w_query1,
+    standard_ref,
+    normed_ref,
+    q_ref,
+    k_ref,
+    v_ref,
+    p_ref,
+    att_ref,
+    ga_ref,
+    gh_ref,
+    hidden_ref,
+    gq_ref,
+    gk_ref,
+    gv_ref,
+    gn_ref,
+    halo_out,
+    grad_halo_out,
+    grad_halo_in,
+    term_ref,
+    rs0,
+    snd1,
+    rs1,
+    acc1,
+    snd2,
+    rs2,
+    acc2,
+    snd3,
+    rs3,
+    full_grad,
+    local_sem,
+    w_send,
+    w_recv,
+    halo_send,
+    halo_recv,
+    rs_send,
+    rs_recv,
+):
+    row_count = lat_rows * lon_cols
+    halo_rows = lat_rows * MARGIN
+    core = lax.axis_index("dp")
+    me = lax.axis_index("fsdp")
+    tile = lax.axis_index("tile")
+    tiles = lax.axis_size("tile")
+    ty, tx = tile // 2, tile % 2
+    x_side = {"tile": tile + 1 - 2 * tx}
+    y_side = {"tile": (tile + 2) % tiles}
+    sibling = {"dp": 1 - core}
+    right = {"tile": (tile + 1) % tiles}
+    left = {"tile": (tile + tiles - 1) % tiles}
+
+    barrier = pltpu.get_barrier_semaphore()
+    partners = [{"tile": (tile + i) % tiles} for i in range(1, 4)]
+    partners += [{"fsdp": (me + i) % fsdp} for i in range(1, fsdp)]
+    partners += [sibling]
+    for partner in partners:
+        pl.semaphore_signal(barrier, inc=1, device_id=partner, device_id_type=pl.DeviceIdType.MESH)
+    pl.semaphore_wait(barrier, len(partners))
+
+    weights = (w_head, w_out0, w_out1, w_key, w_value, w_query0, w_query1)
+
+    def own_piece(chunk):
+        if chunk == HEAD:
+            return head_ref.at[core, ty, tx]
+        if chunk == OUT0:
+            return out_ref.at[ty, tx, :, pl.ds(pl.multiple_of(core * 2 * HALF, 128), HALF)]
+        if chunk == OUT1:
+            return out_ref.at[ty, tx, :, pl.ds(pl.multiple_of(core * 2 * HALF + HALF, 128), HALF)]
+        start, size = {
+            KEY: (INNER, INNER),
+            VALUE: (2 * INNER, INNER),
+            QUERY0: (0, HALF),
+            QUERY1: (HALF, HALF),
+        }[chunk]
+        return qkv_ref.at[core, ty, tx, :, pl.ds(start, size)]
+
+    def remote(src, dst, send, recv, device):
+        return pltpu.make_async_remote_copy(
+            src_ref=src,
+            dst_ref=dst,
+            send_sem=send,
+            recv_sem=recv,
+            device_id=device,
+            device_id_type=pl.DeviceIdType.MESH,
+        )
+
+    def weight_copy(chunk, stage, k):
+        full = weights[chunk]
+        send, recv = w_send.at[chunk, stage, k - 1], w_recv.at[chunk, stage, k - 1]
+        source = (me + fsdp - k) % fsdp
+        if stage == 0:
+            return remote(
+                own_piece(chunk),
+                full.at[me, core, ty, tx],
+                send,
+                recv,
+                {"fsdp": (me + k) % fsdp},
+            )
+        if stage == 1:
+            part = full.at[source, core, ty, tx]
+            device = x_side if ROUTES[chunk] == 0 else y_side
+        elif stage == 2:
+            if ROUTES[chunk] == 0:
+                part, device = full.at[source, core, ty], y_side
+            else:
+                part, device = full.at[source, core, :, tx], x_side
+        else:
+            part, device = full.at[source, core], sibling
+        return remote(part, part, send, recv, device)
+
+    def advance(chunk, stage):
+        for k in range(1, fsdp):
+            if stage > 0:
+                weight_copy(chunk, stage - 1, k).wait_recv()
+            if stage < 4:
+                weight_copy(chunk, stage, k).start()
+
+    def local_copies():
+        pairs = [(head_ref, w_head.at[me])]
+        for d in range(2):
+            for half, full in enumerate((w_out0, w_out1)):
+                start = d * 2 * HALF + half * HALF
+                pairs.append((out_ref.at[:, :, :, pl.ds(start, HALF)], full.at[me, d]))
+        for full, start, size in (
+            (w_key, INNER, INNER),
+            (w_value, 2 * INNER, INNER),
+            (w_query0, 0, HALF),
+            (w_query1, HALF, HALF),
+        ):
+            pairs.append((qkv_ref.at[:, :, :, :, pl.ds(start, size)], full.at[me]))
+        return [
+            pltpu.make_async_copy(src, dst, local_sem.at[i]) for i, (src, dst) in enumerate(pairs)
+        ]
+
+    for chunk in range(7):
+        advance(chunk, 0)
+    copies = local_copies()
+    for copy in copies:
+        copy.start()
+
+    scale = HEAD_DIM ** (-0.5)
+
+    values = tokens_ref[...].astype(jnp.float32)
+    average = jnp.mean(values, axis=-1, keepdims=True)
+    centred = values - average
+    variance = jnp.mean(centred * centred, axis=-1, keepdims=True)
+    inverse_dev = lax.rsqrt(variance + EPSILON)
+    standard = centred * inverse_dev
+    standard_ref[...] = standard
+    normed_ref[...] = (standard * gain_ref[...]).astype(jnp.bfloat16)
+
+    def mat(ref, columns):
+        return ref[...].reshape(-1, columns)
+
+    advance(HEAD, 1)
+    advance(OUT0, 1)
+    advance(OUT1, 1)
+    advance(HEAD, 2)
+    advance(OUT0, 2)
+    advance(OUT1, 2)
+    advance(KEY, 1)
+    advance(VALUE, 1)
+    advance(HEAD, 3)
+    advance(OUT0, 3)
+    advance(OUT1, 3)
+    advance(QUERY0, 1)
+    advance(QUERY1, 1)
+    advance(KEY, 2)
+    advance(VALUE, 2)
+    for copy in copies:
+        copy.wait()
+    advance(HEAD, 4)
+    depth = w_head.shape[1] * 4 * w_head.shape[4]
+
+    def grad_hidden_step(f, _):
+        rows = w_head[f].reshape(depth, HEAD_OUT)
+        gh_ref[:, pl.ds(pl.multiple_of(f * depth, 128), depth)] = dot_nt(grad_rows_ref[...], rows)
+        return 0
+
+    lax.fori_loop(0, fsdp, grad_hidden_step, 0)
+    advance(OUT0, 4)
+    advance(OUT1, 4)
+    out_parts = [(d, half) for d in range(2) for half in range(2)]
+
+    def out_block(d, half):
+        full = (w_out0, w_out1)[half]
+        return full[:, d].reshape(INNER, HALF)
+
+    def out_columns(d, half):
+        return pl.ds(d * 2 * HALF + half * HALF, HALF)
+
+    grad_attended = jnp.zeros((row_count, INNER), jnp.float32)
+    for d, half in out_parts:
+        low = gh_ref[:, out_columns(d, half)].astype(jnp.bfloat16)
+        grad_attended = grad_attended + dot_nt(low, out_block(d, half))
+    ga_ref[...] = grad_attended.astype(jnp.bfloat16)
+
+    advance(KEY, 3)
+    advance(VALUE, 3)
+    advance(QUERY0, 2)
+    advance(QUERY1, 2)
+
+    def edge(rows, first):
+        shaped = rows.reshape(lat_rows, lon_cols, rows.shape[-1])
+        part = shaped[:, :MARGIN] if first else shaped[:, lon_cols - MARGIN :]
+        return part.reshape(halo_rows, rows.shape[-1])
+
+    def halo_copy(which, side):
+        full = (k_ref, v_ref)[which]
+        dst = full.at[pl.ds(row_count + side * halo_rows, halo_rows)]
+        return remote(
+            halo_out.at[which, side],
+            dst,
+            halo_send.at[which, side],
+            halo_recv.at[which, side],
+            (right, left)[side],
+        )
+
+    step_columns = 256
+
+    def project(full, which):
+        target = (k_ref, v_ref)[which]
+
+        def step(j, _):
+            columns = pl.ds(pl.multiple_of(j * step_columns, 128), step_columns)
+            rows = full[:, :, :, :, :, columns].reshape(-1, step_columns)
+            product = dot_nn(normed_ref[...], rows)
+            target[pl.ds(0, row_count), columns] = product.astype(jnp.bfloat16)
+            halo_out[which, 0, :, columns] = edge(product, False).astype(jnp.bfloat16)
+            halo_out[which, 1, :, columns] = edge(product, True).astype(jnp.bfloat16)
+            return 0
+
+        lax.fori_loop(0, INNER // step_columns, step, 0)
+        for side in range(2):
+            halo_copy(which, side).start()
+
+    advance(KEY, 4)
+    project(w_key, 0)
+    advance(QUERY0, 3)
+    advance(QUERY1, 3)
+    advance(VALUE, 4)
+    project(w_value, 1)
+    advance(QUERY0, 4)
+    q_ref[:, pl.ds(0, HALF)] = dot_nn(normed_ref[...], mat(w_query0, HALF)).astype(jnp.bfloat16)
+    advance(QUERY1, 4)
+    q_ref[:, pl.ds(HALF, HALF)] = dot_nn(normed_ref[...], mat(w_query1, HALF)).astype(jnp.bfloat16)
+    for which in range(2):
+        for side in range(2):
+            halo_copy(which, side).wait_recv()
+
+    def windows():
+        for i in range(GROUP):
+            low, high = i * HEAD_DIM, (i + 1) * HEAD_DIM
+            start, stop = low // 128 * 128, -(-high // 128) * 128
+            lanes = lax.broadcasted_iota(jnp.int32, (1, stop - start), 1) + start
+            mask = ((lanes >= low) & (lanes < high)).astype(jnp.float32)
+            yield i, start, stop, mask
+
+    def forward(g, _):
+        columns = pl.ds(pl.multiple_of(g * GROUP_WIDTH, 128), GROUP_WIDTH)
+        queries, keys, vals = q_ref[:, columns], k_ref[:, columns], v_ref[:, columns]
+        parts = [None] * (GROUP_WIDTH // 128)
+        for i, start, stop, mask in windows():
+            masked = queries[:, start:stop] * mask.astype(jnp.bfloat16)
+            scores = dot_nt(masked, keys[:, start:stop]) * scale
+            biggest = jnp.max(scores, axis=-1, keepdims=True)
+            exponent = jnp.exp(scores - biggest)
+            softmax = exponent / jnp.sum(exponent, axis=-1, keepdims=True)
+            p_ref[g * GROUP + i] = softmax
+            product = dot_nn(softmax.astype(jnp.bfloat16), vals[:, start:stop]) * mask
+            add_parts(parts, start, product)
+        att_ref[:, columns] = jnp.concatenate(parts, axis=1).astype(jnp.bfloat16)
+        return 0
+
+    def add_parts(parts, start, product):
+        for j in range(product.shape[1] // 128):
+            piece = product[:, j * 128 : (j + 1) * 128]
+            at = start // 128 + j
+            parts[at] = piece if parts[at] is None else parts[at] + piece
+
+    lax.fori_loop(0, HEADS // GROUP, forward, 0)
+    for d, half in out_parts:
+        columns = out_columns(d, half)
+        mixed = dot_nn(att_ref[...], out_block(d, half))
+        hidden_ref[:, columns] = (tokens_ref[:, columns].astype(jnp.float32) + mixed).astype(
+            jnp.bfloat16
+        )
+
+    def term_step(f, _):
+        part = hidden_ref[:, pl.ds(pl.multiple_of(f * depth, 128), depth)]
+        term_ref[f] = dot_tn(part, grad_rows_ref[...]).reshape(term_ref.shape[1:])
+        return 0
+
+    lax.fori_loop(0, fsdp, term_step, 0)
+
+    core_copy = remote(term_ref.at[:, 1 - core], rs0, rs_send.at[0], rs_recv.at[0], sibling)
+    y_copy = remote(snd1, rs1, rs_send.at[1], rs_recv.at[1], y_side)
+    x_copy = remote(snd2, rs2, rs_send.at[2], rs_recv.at[2], x_side)
+    z_copies = [
+        remote(
+            snd3.at[(me + k) % fsdp],
+            rs3.at[k - 1],
+            rs_send.at[5 + k],
+            rs_recv.at[5 + k],
+            {"fsdp": (me + k) % fsdp},
+        )
+        for k in range(1, fsdp)
+    ]
+    back = [
+        remote(full_grad.at[core, ty, tx], full_grad.at[core, ty, tx], rs_send.at[3], rs_recv.at[3], x_side),
+        remote(full_grad.at[core, ty], full_grad.at[core, ty], rs_send.at[4], rs_recv.at[4], y_side),
+        remote(full_grad.at[core], full_grad.at[core], rs_send.at[5], rs_recv.at[5], sibling),
+    ]
+
+    core_copy.start()
+    head_out_ref[...] = dot_nn(hidden_ref[...], mat(w_head, HEAD_OUT))
+
+    def backward(g, _):
+        columns = pl.ds(pl.multiple_of(g * GROUP_WIDTH, 128), GROUP_WIDTH)
+        queries, keys, vals = q_ref[:, columns], k_ref[:, columns], v_ref[:, columns]
+        grads = ga_ref[:, columns]
+        query_parts = [None] * (GROUP_WIDTH // 128)
+        key_parts = [None] * (GROUP_WIDTH // 128)
+        value_parts = [None] * (GROUP_WIDTH // 128)
+        for i, start, stop, mask in windows():
+            softmax = p_ref[g * GROUP + i]
+            masked = grads[:, start:stop] * mask.astype(jnp.bfloat16)
+            weights_grad = dot_nt(masked, vals[:, start:stop])
+            weighted = jnp.sum(softmax * weights_grad, axis=-1, keepdims=True)
+            grad_scores = (softmax * (weights_grad - weighted)).astype(jnp.bfloat16)
+            add_parts(query_parts, start, dot_nn(grad_scores, keys[:, start:stop]) * (mask * scale))
+            add_parts(
+                key_parts, start, dot_tn(grad_scores, queries[:, start:stop]) * (mask * scale)
+            )
+            add_parts(
+                value_parts,
+                start,
+                dot_tn(softmax.astype(jnp.bfloat16), grads[:, start:stop]) * mask,
+            )
+        gq_ref[:, columns] = jnp.concatenate(query_parts, axis=1).astype(jnp.bfloat16)
+        gk_ref[:, columns] = jnp.concatenate(key_parts, axis=1)
+        gv_ref[:, columns] = jnp.concatenate(value_parts, axis=1)
+        return 0
+
+    lax.fori_loop(0, 1, backward, 0)
+
+    core_copy.wait_recv()
+    snd1[...] = (term_ref[:, core, 1 - ty] + rs0[:, 1 - ty]).astype(jnp.bfloat16)
+    y_copy.start()
+    acc1[...] = term_ref[:, core, ty] + rs0[:, ty]
+
+    lax.fori_loop(1, HEADS // GROUP, backward, 0)
+
+    def grad_halo_copy(which, side):
+        return remote(
+            grad_halo_out.at[which, side],
+            grad_halo_in.at[which, side],
+            halo_send.at[2 + which, side],
+            halo_recv.at[2 + which, side],
+            (left, right)[side],
+        )
+
+    for which, full in enumerate((gk_ref, gv_ref)):
+        for side in range(2):
+            rows = full[pl.ds(row_count + side * halo_rows, halo_rows), :]
+            grad_halo_out[which, side] = rows.astype(jnp.bfloat16)
+            grad_halo_copy(which, side).start()
+
+    y_copy.wait_recv()
+    snd2[...] = (acc1[:, 1 - tx] + rs1[:, 1 - tx].astype(jnp.float32)).astype(jnp.bfloat16)
+    x_copy.start()
+    acc2[...] = acc1[:, tx] + rs1[:, tx].astype(jnp.float32)
+
+    def columns_of(f):
+        return pl.ds(pl.multiple_of(f * depth, 128), depth)
+
+    def grad_query_step(f, _):
+        total = dot_nt(gq_ref[:, pl.ds(0, HALF)], w_query0[f].reshape(depth, HALF))
+        total += dot_nt(gq_ref[:, pl.ds(HALF, HALF)], w_query1[f].reshape(depth, HALF))
+        gn_ref[:, columns_of(f)] = total
+        return 0
+
+    lax.fori_loop(0, fsdp, grad_query_step, 0)
+
+    x_copy.wait_recv()
+    acc2[...] = acc2[...] + rs2[...].astype(jnp.float32)
+    snd3[...] = acc2[...].astype(jnp.bfloat16)
+    for copy in z_copies:
+        copy.start()
+
+    def own_cells(which):
+        full = (gk_ref, gv_ref)[which]
+        for side in range(2):
+            grad_halo_copy(which, side).wait_recv()
+        rows = full[pl.ds(0, row_count), :].reshape(lat_rows, lon_cols, INNER)
+        shape = (lat_rows, MARGIN, INNER)
+        last = grad_halo_in[which, 0].astype(jnp.float32).reshape(shape)
+        first = grad_halo_in[which, 1].astype(jnp.float32).reshape(shape)
+        rows = jnp.concatenate(
+            [
+                rows[:, :MARGIN] + first,
+                rows[:, MARGIN : lon_cols - MARGIN],
+                rows[:, lon_cols - MARGIN :] + last,
+            ],
+            axis=1,
+        )
+        return rows.reshape(row_count, INNER).astype(jnp.bfloat16)
+
+    def add_pair(which, full):
+        k_ref[pl.ds(0, row_count), :] = own_cells(which)
+
+        def step(f, _):
+            columns = columns_of(f)
+            gn_ref[:, columns] += dot_nt(
+                k_ref[pl.ds(0, row_count), :], full[f].reshape(depth, INNER)
+            )
+            return 0
+
+        lax.fori_loop(0, fsdp, step, 0)
+
+    add_pair(0, w_key)
+    for copy in z_copies:
+        copy.wait_recv()
+    summed = acc2[me]
+    for k in range(1, fsdp):
+        summed = summed + rs3[k - 1].astype(jnp.float32)
+    full_grad[core, ty, tx] = summed
+    back[0].start()
+    add_pair(1, w_value)
+    back[0].wait_recv()
+    back[1].start()
+
+    values = tokens_ref[...].astype(jnp.float32)
+    average = jnp.mean(values, axis=-1, keepdims=True)
+    centred = values - average
+    inverse_dev = lax.rsqrt(jnp.mean(centred * centred, axis=-1, keepdims=True) + EPSILON)
+    grad_input = norm_backward(gn_ref[...], standard_ref[...], inverse_dev, gain_ref[...])
+    grad_tokens_ref[...] = (gh_ref[...] + grad_input).astype(jnp.bfloat16)
+
+    back[1].wait_recv()
+    back[2].start()
+    back[2].wait_recv()
+    grad_head_ref[...] = full_grad[...]
+
+    for chunk in range(7):
+        for stage in range(4):
+            for k in range(1, fsdp):
+                weight_copy(chunk, stage, k).wait_send()
+    for which in range(2):
+        for side in range(2):
+            halo_copy(which, side).wait_send()
+            grad_halo_copy(which, side).wait_send()
+    for copy in [core_copy, y_copy, x_copy] + z_copies + back:
+        copy.wait_send()
+
+
+def fused_block(tokens, norm_gain, qkv, out_weight, head_weight, grad_rows, lat_rows, lon_cols):
+    fsdp = lax.axis_size("fsdp")
+    row_count = lat_rows * lon_cols
+    halo_rows = lat_rows * MARGIN
+    key_count = row_count + 2 * halo_rows
+    piece = qkv.shape[0] // 8
+    out_piece = out_weight.shape[0] // 4
+    bf16, f32 = jnp.bfloat16, jnp.float32
+    vmem = pl.BlockSpec(memory_space=pltpu.VMEM)
+    hbm = pl.BlockSpec(memory_space=pl.ANY)
+
+    def full(rows, columns):
+        return pltpu.VMEM((fsdp, 2, 2, 2, rows, columns), bf16)
+
+    head_out, grad_tokens, grad_head = pl.pallas_call(
+        functools.partial(block_kernel, fsdp, lat_rows, lon_cols),
+        out_shape=(
+            jax.ShapeDtypeStruct((row_count, HEAD_OUT), f32),
+            jax.ShapeDtypeStruct((row_count, D), bf16),
+            jax.ShapeDtypeStruct((2, 2, 2, piece, HEAD_OUT), f32),
+        ),
+        in_specs=[vmem, vmem, hbm, hbm, hbm, vmem],
+        out_specs=(vmem, vmem, vmem),
+        scratch_shapes=[
+            full(piece, HEAD_OUT),
+            full(out_piece, HALF),
+            full(out_piece, HALF),
+            full(piece, INNER),
+            full(piece, INNER),
+            full(piece, HALF),
+            full(piece, HALF),
+            pltpu.VMEM((row_count, D), f32),
+            pltpu.VMEM((row_count, D), bf16),
+            pltpu.VMEM((row_count, INNER), bf16),
+            pltpu.VMEM((key_count, INNER), bf16),
+            pltpu.VMEM((key_count, INNER), bf16),
+            pltpu.VMEM((HEADS, row_count, key_count), f32),
+            pltpu.VMEM((row_count, INNER), bf16),
+            pltpu.VMEM((row_count, INNER), bf16),
+            pltpu.VMEM((row_count, D), f32),
+            pltpu.VMEM((row_count, D), bf16),
+            pltpu.VMEM((row_count, INNER), bf16),
+            pltpu.VMEM((key_count, INNER), f32),
+            pltpu.VMEM((key_count, INNER), f32),
+            pltpu.VMEM((row_count, D), f32),
+            pltpu.VMEM((2, 2, halo_rows, INNER), bf16),
+            pltpu.VMEM((2, 2, halo_rows, INNER), bf16),
+            pltpu.VMEM((2, 2, halo_rows, INNER), bf16),
+            pltpu.VMEM((fsdp, 2, 2, 2, piece, HEAD_OUT), f32),
+            pltpu.VMEM((fsdp, 2, 2, piece, HEAD_OUT), f32),
+            pltpu.VMEM((fsdp, 2, piece, HEAD_OUT), bf16),
+            pltpu.VMEM((fsdp, 2, piece, HEAD_OUT), bf16),
+            pltpu.VMEM((fsdp, 2, piece, HEAD_OUT), f32),
+            pltpu.VMEM((fsdp, piece, HEAD_OUT), bf16),
+            pltpu.VMEM((fsdp, piece, HEAD_OUT), bf16),
+            pltpu.VMEM((fsdp, piece, HEAD_OUT), f32),
+            pltpu.VMEM((fsdp, piece, HEAD_OUT), bf16),
+            pltpu.VMEM((fsdp - 1, piece, HEAD_OUT), bf16),
+            pltpu.VMEM((2, 2, 2, piece, HEAD_OUT), f32),
+            pltpu.SemaphoreType.DMA((9,)),
+            pltpu.SemaphoreType.DMA((7, 4, fsdp - 1)),
+            pltpu.SemaphoreType.DMA((7, 4, fsdp - 1)),
+            pltpu.SemaphoreType.DMA((4, 2)),
+            pltpu.SemaphoreType.DMA((4, 2)),
+            pltpu.SemaphoreType.DMA((5 + fsdp,)),
+            pltpu.SemaphoreType.DMA((5 + fsdp,)),
+        ],
+        compiler_params=pltpu.CompilerParams(
+            collective_id=0, has_side_effects=True, vmem_limit_bytes=56 * 1024 * 1024
+        ),
+        cost_estimate=pl.CostEstimate(
+            flops=int(7e9), bytes_accessed=int(1e7), transcendentals=row_count * key_count * HEADS
+        ),
+    )(
+        tokens,
+        norm_gain.reshape(1, D),
+        qkv.reshape(2, 2, 2, piece, qkv.shape[1]),
+        out_weight.reshape(2, 2, out_piece, D),
+        head_weight.reshape(2, 2, 2, piece, HEAD_OUT),
+        grad_rows,
+    )
+    return head_out, grad_tokens, grad_head.reshape(8 * piece, HEAD_OUT)
+
+
+def fine_residual(coarse, lat_rows, lon_cols):
+    coarse_padded_grid = with_halo(coarse, (("tile", 2),), 1)
+    lat_lower, lat_upper_weight = interp_weights(jnp.arange(4 * lat_rows, dtype=jnp.int32))
+    latitude_matrix = build_matrix(
+        jnp.clip(lat_lower, 0, lat_rows - 1),
+        jnp.clip(lat_lower + 1, 0, lat_rows - 1),
+        lat_upper_weight,
+        lat_rows,
+    )
+    lon_lower, lon_upper_weight = interp_weights(jnp.arange(4 * lon_cols, dtype=jnp.int32))
+    lon_matrix = build_matrix(lon_lower + 1, lon_lower + 2, lon_upper_weight, lon_cols + 2)
+    incomplete_grid = jnp.einsum(
+        "lj,kji->kli", latitude_matrix, coarse_padded_grid, precision=lax.Precision.HIGHEST
+    )
+    return jnp.einsum(
+        "vrb,cb->vrc", incomplete_grid, lon_matrix, precision=lax.Precision.HIGHEST
+    )
+
+
+def fused_shards(
+    tokens, norm_gain, query_key_value_weight, out_weight, head_weight, coarse, grad_fine
+):
+    lat_rows = tokens.shape[1]
+    lon_cols = tokens.shape[2]
+    row_count = lat_rows * lon_cols
+    grad_rows = (
+        grad_fine[0]
+        .astype(jnp.bfloat16)
+        .reshape(VARS, lat_rows, 4, lon_cols, 4)
+        .transpose(1, 3, 0, 2, 4)
+        .reshape(row_count, HEAD_OUT)
+    )
+    residual = fine_residual(coarse[0], lat_rows, lon_cols)
+    head_out, grad_tokens, grad_head = fused_block(
+        tokens[0].reshape(row_count, D),
+        norm_gain,
+        query_key_value_weight,
+        out_weight,
+        head_weight,
+        grad_rows,
+        lat_rows,
+        lon_cols,
+    )
+    fine_head = (
+        head_out.reshape(lat_rows, lon_cols, VARS, 4, 4)
+        .transpose(2, 0, 3, 1, 4)
+        .reshape(VARS, 4 * lat_rows, 4 * lon_cols)
+    )
+    fine_grid = fine_head + residual
+    return (fine_grid[None], grad_tokens.reshape(1, lat_rows, lon_cols, D), grad_head)
+
+
+def fits_pieces(mesh):
+    dp, fsdp, tile = (mesh.shape[axis] for axis in ("dp", "fsdp", "tile"))
+    if dp != 2 or tile != 4 or fsdp < 2:
+        return False
+    return D % (fsdp * 128) == 0 and INNER % (fsdp * 64) == 0
 
 
 def shards(tokens, norm_gain, query_key_value_weight, out_weight, head_weight, coarse, grad_fine):
@@ -210,7 +854,7 @@
         P(("dp", "fsdp"), None, None, "tile"),
     )
     return jax.shard_map(
-        shards,
+        fused_shards if fits_pieces(mesh) else shards,
         mesh=mesh,
         in_specs=placed,
         out_specs=(

time: 353 us -> 127 us (0.36)
  waiting for transfers between devices: 202 us -> 0.01 us
  Pallas kernels: 0 us -> 104 us
  matrix products: 38.3 us -> 2.51 us
  blocking collectives: 35.7 us -> 0 us
  local copies, waits for them, and re-layouts: 40.8 us -> 13.7 us
  between operations: 14.1 us -> 0.74 us
  other arithmetic: 12.1 us -> 1.03 us
  starting transfers between devices: 9.31 us -> 3.9 us
    all_gather x2 -> x0, waiting for transfers between devices: 137 us -> none  [the longest x1 95.1 us: shards(): lax.all_gather(query_key_value_weight, 'fsdp', axis=0, tiled=True)]
    pallas_call x0 -> x1, Pallas kernels: none -> 104 us  [fused_block(): pl.pallas_call(functools.partial(block_kernel, fsdp, lat_rows, lon_cols),...]
    psum x1 -> x0, waiting for transfers between devices: 49.3 us -> none  [shards(): grad_head = lax.psum(head_block, ('dp', 'tile'))]
    all_gather x1 -> x0, blocking collectives: 35.7 us -> none  [shards(): full_head = lax.all_gather(head_weight, 'fsdp', axis=0, tiled=True)]
    dot_general x14 -> x2, matrix products: 34.2 us -> 2.51 us  [the longest x1 1.37 us: fine_residual(): jnp.einsum('lj,kji->kli', latitude_matrix, coarse_padded_grid, precision=...]
    ppermute x2 -> x0, waiting for transfers between devices: 15.2 us -> none  [from_behind(): return lax.ppermute(value, axis, pairs)]
    convert_element_type x5 -> x1, other arithmetic: 9.05 us -> 1 us  [fused_shards(): grad_rows = grad_fine[0].astype(jnp.bfloat16).reshape(VARS, lat_rows, 4,...]
    unnamed x54 -> x9, local copies, waits for them, and re-layouts: 11.2 us -> 4.07 us
  transfers between devices with their start and end apart: 10 -> 2, of which waited for: 5 -> 0; matrix products, arithmetic and copies ran while one was open for 16% -> 9% of each run, Pallas kernels for 0% -> 83%
where the time goes in v1:
time: 127 us; the launch traced here: 126 us
  Pallas kernels  104 us (82%)
  local copies, waits for them, and re-layouts  13.7 us (11%)
  starting transfers between devices  3.9 us (3%)
  matrix products  2.51 us (2%)
    pallas_call x1, Pallas kernels, fused_block(): pl.pallas_call(functools.partial(block_kernel, fsdp, lat_rows, lon_cols),...  104 us
    unnamed x9, local copies, waits for them, and re-layouts  4.07 us
    ppermute x1, starting transfers between devices, with_halo(): after = lax.ppermute(leading, axis, down)  3.89 us
  transfers between devices with their start and end apart: 2, of which 0 were waited for; matrix products, arithmetic and copies ran while one was open for 9% of the time, Pallas kernels for 83%

profile of v1, /device:TPU:0, one launch (start us, length us, event | category | flops | bytes accessed | tf_op | source)
XLA Modules:
  0.0 126.2 jit_solution(16945603216970955232)
XLA Ops:
  0.6 1.7 %fusion.31 = (f32[20,8,1]{2,1,0:T(8,128)}, f32[20,8,1]{2,1,0:T(8,128)}) fusion(f32[20,8,32]{2,1,0:T(8,128)} %bitcast.33), kind=kLoop, calls=%fused_computation.59 | loop fusion | bytes 2560 | tf_op jit(solution)/shard_map/slice | solution.py:27
  2.3 3.9 %collective-permute-start.1 = (f32[20,8,1]{2,1,0:T(8,128)}, f32[20,8,1]{2,1,0:T(8,128)S(1)}, u32[]{:S(2)}, u32[]{:S(2)}) collective-permute-start(f32[20,8,1]{2,1,0:T(8,128)} %get-tuple-element.16), channel_id=1, source_target_pairs={{1,0},{2,1},{3,2},{0,3},{5,4},{6,5},{7,6},{4,7},{9,8},{10,9},{11,1... | collective-permute-start | bytes 1928 | tf_op jit(solution)/shard_map/ppermute | solution.py:30
  6.2 0.0 collective-permute-start
  6.3 1.3 %reshape.115.gain_ref = f32[1,1536]{1,0:T(1,128)} reshape(f32[1536]{0:T(1024)} %param.8) | data formatting | bytes 12288 | tf_op jit(solution)/shard_map/reshape | solution.py:703
  7.6 1.8 %copy.14 = bf16[384,320]{1,0:T(8,128)(2,1)} copy(bf16[384,320]{0,1:T(8,128)(2,1)} %param.11) | data formatting | bytes 491520 | tf_op args[4]
  9.4 1.0 convert_element_type.47
  10.4 0.5 copy.15
  10.9 1.5 %copy.16 = bf16[8,32,20,4,4]{1,0,4,3,2:T(8,128)(2,1)S(1)} copy(bf16[8,32,20,4,4]{2,4,1,3,0:T(4,128)(2,1)S(1)} %bitcast.31) | data formatting | bytes 327680 | tf_op jit(solution)/shard_map/transpose | solution.py:741
  12.4 0.4 reshape.119
  12.8 0.8 copy.17.grad_rows_ref
  13.7 104.4 %shard_map.94 = (f32[256,320]{1,0:T(8,128)}, bf16[256,1536]{1,0:T(8,128)(2,1)}, f32[2,2,2,48,320]{4,3,2,1,0:T(8,128)}) custom-call(bf16[256,1536]{1,0:T(8,128)(2,1)} %bitcast.38, f32[1,1536]{1,0:T(1,128)} %reshape.115.gain_ref, bf16[2,2,2,48,2304]{4,3,2,1,0:T(8,128)(2,1)} %bitcast.37, bf16[2,2,48,1536]{3,2,1,0:T(8,128)(2,1)} %bitcast.39, ...), custom_call_target="tpu_custom_call" | custom-call | flops 7000000000 | bytes 10000000 | tf_op jit(solution)/shard_map/pallas_call | solution.py:642
  118.1 1.1 copy.18
  119.2 0.3 reshape.120
  119.5 1.2 copy.19
  120.8 0.0 copy-start.2
  120.8 0.0 copy-start.1
  120.8 0.7 copy.20
  121.5 0.0 copy-start
  121.5 0.4 copy-done.2
  121.8 1.0 copy.21
  122.8 0.0 collective-permute-done.1
  122.8 0.0 collective-permute-done
  122.8 0.0 copy-done.1
  122.8 1.4 %convolution_bitcast_fusion = f32[20,32,34]{2,1,0:T(8,128)S(1)} fusion(f32[20,8,1]{2,1,0:T(8,128)S(1)} %collective-permute-done.1, f32[20,8,32]{2,1,0:T(8,128)S(1)} %bitcast.34, f32[20,8,1]{2,1,0:T(8,128)} %collective-permute-done, f32[32]{0:T(128)S(1)} %get-tuple-element.19, s32[32]{0:T(128)S(1)} %get-tuple-element.17, f32[32]{0:T(128)S(1)} %get-tuple-element.20, ...), kind=kOutput, calls=%fused_computation.2 | convolution fusion | flops 2101120 | bytes 109312 | tf_op jit(solution)/shard_map/lj,kji->kli/dot_general | solution.py:723
  124.2 1.1 fusion
  125.3 0.0 copy-done
  125.4 0.9 copy.23
  (4 shorter events, 0.0 us)
Async XLA Ops:
  2.3 120.5 %collective-permute-start.1 = (f32[20,8,1]{2,1,0:T(8,128)}, f32[20,8,1]{2,1,0:T(8,128)S(1)}, u32[]{:S(2)}, u32[]{:S(2)}) collective-permute-start(f32[20,8,1]{2,1,0:T(8,128)} %get-tuple-element.16), channel_id=1, source_target_pairs={{1,0},{2,1},{3,2},{0,3},{5,4},{6,5},{7,6},{4,7},{9,8},{10,9},{11,1... | collective-permute-start | bytes 1928 | tf_op jit(solution)/shard_map/ppermute | solution.py:30
  6.2 116.6 %collective-permute-start = (f32[20,8,1]{2,1,0:T(8,128)}, f32[20,8,1]{2,1,0:T(8,128)}, u32[]{:S(2)}, u32[]{:S(2)}) collective-permute-start(f32[20,8,1]{2,1,0:T(8,128)} %get-tuple-element.15), channel_id=1, source_target_pairs={{0,1},{1,2},{2,3},{3,0},{4,5},{5,6},{6,7},{7,4},{8,9},{9,10},{10,1... | collective-permute-start | bytes 1928 | tf_op jit(solution)/shard_map/ppermute | solution.py:29
  120.8 1.1 copy-start.2
  120.8 2.1 %copy-start.1 = (f32[1,20,8,32]{3,2,1,0:T(8,128)S(1)}, f32[1,20,8,32]{3,2,1,0:T(8,128)}, u32[]{:S(2)}) copy-start(f32[1,20,8,32]{3,2,1,0:T(8,128)} %param.12) | copy-start | bytes 61444
  121.5 3.9 %copy-start = (bf16[256,1536]{1,0:T(8,128)(2,1)S(1)}, bf16[256,1536]{1,0:T(8,128)(2,1)}, u32[]{:S(2)}) copy-start(bf16[256,1536]{1,0:T(8,128)(2,1)} %get-tuple-element.7) | copy-start | bytes 2359300

commit v2 on v0

--- a/solution.py
+++ b/solution.py
@@ -1,6 +1,10 @@
+import functools
+
 import jax
 import jax.numpy as jnp
 from jax import lax
+from jax.experimental import pallas as pl
+from jax.experimental.pallas import tpu as pltpu
 from jax.sharding import PartitionSpec as P
 
 D = 1536
@@ -122,6 +126,727 @@
     return lax.dot_general(
         left_side, right_side, (((1,), (1,)), ((), ())), preferred_element_type=jnp.float32
     )
+
+
+def dot_nt(left_side, right_side):
+    return lax.dot_general(
+        left_side, right_side, (((1,), (1,)), ((), ())), preferred_element_type=jnp.float32
+    )
+
+
+def dot_tn(left_side, right_side):
+    return lax.dot_general(
+        left_side, right_side, (((0,), (0,)), ((), ())), preferred_element_type=jnp.float32
+    )
+
+
+def dot_nn(left_side, right_side):
+    return jnp.dot(left_side, right_side, preferred_element_type=jnp.float32)
+
+
+OUT0, OUT1, HEAD = range(3)
+KEY, VALUE, QUERY = range(3)
+CHUNKS = 9
+ROUTES = (0, 1, 0, 0, 1, 0, 1, 0, 1)
+HALF = INNER // 2
+GROUPS = 2
+GROUP = HEADS // GROUPS
+PADDED = 32
+
+
+def split_dot(dot, left_side, right_side):
+    first = left_side.astype(jnp.bfloat16)
+    remainder = left_side - first.astype(jnp.float32)
+    second = remainder.astype(jnp.bfloat16)
+    third = (remainder - second.astype(jnp.float32)).astype(jnp.bfloat16)
+    return dot(third, right_side) + dot(second, right_side) + dot(first, right_side)
+
+
+def spread(rows, columns, where):
+    row = lax.broadcasted_iota(jnp.int32, (rows, columns), 0)
+    column = lax.broadcasted_iota(jnp.int32, (rows, columns), 1)
+    return where(row, column)
+
+
+def block_kernel(
+    fsdp,
+    lat_rows,
+    lon_cols,
+    tokens_ref,
+    gain_ref,
+    qkv_ref,
+    out_ref,
+    head_ref,
+    coarse_ref,
+    fine_grad_ref,
+    fine_ref,
+    grad_tokens_ref,
+    grad_head_ref,
+    w_out0,
+    w_out1,
+    w_head,
+    w_key0,
+    w_value0,
+    w_query0,
+    w_key1,
+    w_value1,
+    w_query1,
+    standard_ref,
+    normed_ref,
+    q_ref,
+    k_ref,
+    v_ref,
+    p_ref,
+    att_ref,
+    ga_ref,
+    gh_ref,
+    hidden_ref,
+    gq_ref,
+    gk_ref,
+    gv_ref,
+    gn_ref,
+    rows_ref,
+    shuffled_ref,
+    residual_ref,
+    coarse_pad,
+    w_head_shuffled,
+    halo_out,
+    grad_halo_out,
+    grad_halo_in,
+    term_ref,
+    rs0,
+    snd1,
+    rs1,
+    acc1,
+    snd2,
+    rs2,
+    acc2,
+    rs3,
+    full_grad,
+    local_sem,
+    w_send,
+    w_recv,
+    halo_send,
+    halo_recv,
+    coarse_send,
+    coarse_recv,
+    rs_send,
+    rs_recv,
+):
+    row_count = lat_rows * lon_cols
+    halo_rows = lat_rows * MARGIN
+    fine_cols = 4 * lon_cols
+    core = lax.axis_index("dp")
+    me = lax.axis_index("fsdp")
+    tile = lax.axis_index("tile")
+    tiles = lax.axis_size("tile")
+    ty, tx = tile // 2, tile % 2
+    x_side = {"tile": tile + 1 - 2 * tx}
+    y_side = {"tile": (tile + 2) % tiles}
+    sibling = {"dp": 1 - core}
+    right = {"tile": (tile + 1) % tiles}
+    left = {"tile": (tile + tiles - 1) % tiles}
+    weights = (w_out0, w_out1, w_head, w_key0, w_value0, w_query0, w_key1, w_value1, w_query1)
+    depth = w_head.shape[1] * 4 * w_head.shape[4]
+    bf16, f32 = jnp.bfloat16, jnp.float32
+
+    def qkv_chunk(group, which):
+        return 3 + 3 * group + which
+
+    def qkv_columns(chunk):
+        group, which = (chunk - 3) // 3, (chunk - 3) % 3
+        return pl.ds({KEY: 1, VALUE: 2, QUERY: 0}[which] * INNER + group * HALF, HALF)
+
+    def own_piece(chunk):
+        if chunk == HEAD:
+            return w_head.at[me, core, ty, tx]
+        if chunk in (OUT0, OUT1):
+            start = core * 2 * HALF + (chunk - OUT0) * HALF
+            return out_ref.at[ty, tx, :, pl.ds(pl.multiple_of(start, 128), HALF)]
+        return qkv_ref.at[core, ty, tx, :, qkv_columns(chunk)]
+
+    def remote(src, dst, send, recv, device):
+        return pltpu.make_async_remote_copy(
+            src_ref=src,
+            dst_ref=dst,
+            send_sem=send,
+            recv_sem=recv,
+            device_id=device,
+            device_id_type=pl.DeviceIdType.MESH,
+        )
+
+    def weight_copy(chunk, stage, k):
+        full = weights[chunk]
+        send, recv = w_send.at[chunk, stage, k - 1], w_recv.at[chunk, stage, k - 1]
+        source = (me + fsdp - k) % fsdp
+        if stage == 0:
+            device = {"fsdp": (me + k) % fsdp}
+            return remote(own_piece(chunk), full.at[me, core, ty, tx], send, recv, device)
+        if stage == 1:
+            part = full.at[source, core, ty, tx]
+            device = x_side if ROUTES[chunk] == 0 else y_side
+        elif stage == 2:
+            if ROUTES[chunk] == 0:
+                part, device = full.at[source, core, ty], y_side
+            else:
+                part, device = full.at[source, core, :, tx], x_side
+        else:
+            part, device = full.at[source, core], sibling
+        return remote(part, part, send, recv, device)
+
+    def advance(*steps):
+        for chunk, stage in steps:
+            for k in range(1, fsdp):
+                if stage > 0:
+                    weight_copy(chunk, stage - 1, k).wait_recv()
+                if stage < 4:
+                    weight_copy(chunk, stage, k).start()
+
+    def local_copies():
+        pairs = []
+        for d in range(2):
+            for half, full in enumerate((w_out0, w_out1)):
+                start = d * 2 * HALF + half * HALF
+                pairs.append((out_ref.at[:, :, :, pl.ds(start, HALF)], full.at[me, d]))
+        for chunk in range(3, CHUNKS):
+            pairs.append((qkv_ref.at[:, :, :, :, qkv_columns(chunk)], weights[chunk].at[me]))
+        return [
+            pltpu.make_async_copy(src, dst, local_sem.at[i]) for i, (src, dst) in enumerate(pairs)
+        ]
+
+    copies = local_copies()
+    for copy in copies:
+        copy.start()
+    eye = spread(depth, depth, lambda r, c: (r == c).astype(f32)).astype(bf16)
+    w_head[me] = dot_nt(eye, head_ref[...]).astype(bf16).reshape(w_head.shape[1:])
+    coarse_pad[pl.ds(MARGIN, lon_cols), :] = coarse_ref[...]
+
+    barrier = pltpu.get_barrier_semaphore()
+    partners = [{"tile": (tile + i) % tiles} for i in range(1, 4)]
+    partners += [{"fsdp": (me + i) % fsdp} for i in range(1, fsdp)]
+    partners += [sibling]
+    for partner in partners:
+        pl.semaphore_signal(barrier, inc=1, device_id=partner, device_id_type=pl.DeviceIdType.MESH)
+    pl.semaphore_wait(barrier, len(partners))
+
+    advance(*[(chunk, 0) for chunk in range(CHUNKS)])
+    coarse_copies = [
+        remote(
+            coarse_pad.at[pl.ds(lon_cols, MARGIN)],
+            coarse_pad.at[pl.ds(0, MARGIN)],
+            coarse_send.at[0],
+            coarse_recv.at[0],
+            right,
+        ),
+        remote(
+            coarse_pad.at[pl.ds(MARGIN, MARGIN)],
+            coarse_pad.at[pl.ds(MARGIN + lon_cols, MARGIN)],
+            coarse_send.at[1],
+            coarse_recv.at[1],
+            left,
+        ),
+    ]
+    for copy in coarse_copies:
+        copy.start()
+
+    scale = HEAD_DIM ** (-0.5)
+
+    def normalised():
+        return layer_norm(tokens_ref[...].astype(f32))
+
+    standard, _ = normalised()
+    standard_ref[...] = standard
+    normed_ref[...] = (standard * gain_ref[...]).astype(bf16)
+
+    advance((OUT0, 1), (OUT1, 1), (HEAD, 1))
+
+    def cell_rows(i, a):
+        return pl.ds((i * 4 + a) * PADDED, VARS)
+
+    def fine_rows(i, a):
+        return pl.ds(4 * i + a, VARS, stride=4 * lat_rows)
+
+    shuffled_ref[...] = jnp.zeros_like(shuffled_ref)
+    for i in range(lat_rows):
+        for a in range(4):
+            shuffled_ref[cell_rows(i, a), :] = fine_grad_ref[fine_rows(i, a), :]
+    by_phase = spread(
+        fine_cols, fine_cols, lambda r, c: (r == 4 * (c % lon_cols) + c // lon_cols).astype(f32)
+    ).astype(bf16)
+    to_phase = spread(
+        fine_cols, fine_cols, lambda r, c: (c == 4 * (r % lon_cols) + r // lon_cols).astype(f32)
+    ).astype(bf16)
+    to_feature = spread(
+        16 * PADDED,
+        HEAD_OUT,
+        lambda r, c: (
+            c == 16 * (r % PADDED) + 4 * (r // PADDED % 4) + r // (4 * PADDED)
+        ).astype(f32),
+    ).astype(bf16)
+    width = 4 * PADDED
+    turned = dot_nn(shuffled_ref[...].astype(bf16), by_phase).T
+    turned = jnp.concatenate(
+        [
+            jnp.concatenate(
+                [
+                    turned[b * lon_cols : (b + 1) * lon_cols, i * width : (i + 1) * width]
+                    for b in range(4)
+                ],
+                axis=1,
+            )
+            for i in range(lat_rows)
+        ],
+        axis=0,
+    )
+    rows_ref[...] = dot_nn(turned.astype(bf16), to_feature).astype(bf16)
+
+    advance((OUT0, 2), (OUT1, 2), (HEAD, 2))
+    advance((3, 1), (4, 1))
+    advance((OUT0, 3), (OUT1, 3), (HEAD, 3))
+    advance((5, 1), (3, 2), (4, 2))
+    for copy in copies:
+        copy.wait()
+
+    def columns_of(f):
+        return pl.ds(pl.multiple_of(f * depth, 128), depth)
+
+    advance((HEAD, 4))
+
+    def grad_hidden_step(f, _):
+        rows = w_head[f].reshape(depth, HEAD_OUT)
+        gh_ref[:, columns_of(f)] = dot_nt(rows_ref[...], rows)
+        w_head_shuffled[pl.ds(pl.multiple_of(f * depth, 128), depth), :] = dot_nt(
+            rows, to_feature
+        ).astype(bf16)
+        return 0
+
+    lax.fori_loop(0, fsdp, grad_hidden_step, 0)
+    advance((6, 1), (5, 2), (3, 3), (4, 3))
+    advance((OUT0, 4), (OUT1, 4))
+    out_parts = [(d, half) for d in range(2) for half in range(2)]
+
+    def out_block(d, half):
+        full = (w_out0, w_out1)[half]
+        return full[:, d].reshape(INNER, HALF)
+
+    def out_columns(d, half):
+        return pl.ds(d * 2 * HALF + half * HALF, HALF)
+
+    grad_attended = jnp.zeros((row_count, INNER), f32)
+    for d, half in out_parts:
+        low = gh_ref[:, out_columns(d, half)].astype(bf16)
+        grad_attended = grad_attended + dot_nt(low, out_block(d, half))
+    ga_ref[...] = grad_attended.astype(bf16)
+
+    advance((7, 1), (6, 2), (5, 3))
+
+    for copy in coarse_copies:
+        copy.wait_recv()
+
+    def lon_weight(row, column):
+        phase = column % 4
+        lower_shift = (phase < 2).astype(jnp.int32)
+        upper_weight = (2 * phase - 3 + 8 * lower_shift).astype(f32) / 8.0
+        lower_cell = column // 4 - lower_shift + MARGIN
+        return jnp.where(row == lower_cell, 1.0 - upper_weight, 0.0) + jnp.where(
+            row == lower_cell + 1, upper_weight, 0.0
+        )
+
+    lon_matrix = spread(coarse_pad.shape[0], fine_cols, lon_weight).astype(bf16)
+    incomplete = split_dot(dot_nn, coarse_pad[...].T, lon_matrix)
+    for i in range(lat_rows):
+        for a in range(4):
+            low = i - 1 if a < 2 else i
+            upper_weight = (5 / 8, 7 / 8, 1 / 8, 3 / 8)[a]
+            lower, upper = (
+                incomplete[cell * PADDED : (cell + 1) * PADDED]
+                for cell in (max(low, 0), min(low + 1, lat_rows - 1))
+            )
+            residual_ref[pl.ds((i * 4 + a) * PADDED, PADDED), :] = (
+                lower * (1.0 - upper_weight) + upper * upper_weight
+            )
+
+    def edge(rows, first):
+        shaped = rows.reshape(lat_rows, lon_cols, rows.shape[-1])
+        part = shaped[:, :MARGIN] if first else shaped[:, lon_cols - MARGIN :]
+        return part.reshape(halo_rows, rows.shape[-1])
+
+    def halo_copy(group, which, side):
+        full = (k_ref, v_ref)[which]
+        index = (0, group, which, side)
+        return remote(
+            halo_out.at[group, which, side],
+            full.at[group, pl.ds(row_count + side * halo_rows, halo_rows)],
+            halo_send.at[index],
+            halo_recv.at[index],
+            (right, left)[side],
+        )
+
+    def grad_halo_copy(group, which, side):
+        index = (1, group, which, side)
+        return remote(
+            grad_halo_out.at[group, which, side],
+            grad_halo_in.at[group, which, side],
+            halo_send.at[index],
+            halo_recv.at[index],
+            (left, right)[side],
+        )
+
+    def project(group, which):
+        full = weights[qkv_chunk(group, which)]
+        product = dot_nn(normed_ref[...], full[...].reshape(-1, HALF))
+        if which == QUERY:
+            q_ref[group] = product.astype(bf16)
+            return
+        (k_ref, v_ref)[which][group, pl.ds(0, row_count)] = product.astype(bf16)
+        for side in range(2):
+            halo_out[group, which, side] = edge(product, side == 1).astype(bf16)
+            halo_copy(group, which, side).start()
+
+    def await_halos(group):
+        for which in range(2):
+            for side in range(2):
+                halo_copy(group, which, side).wait_recv()
+
+    def window(i):
+        low, high = i * HEAD_DIM, (i + 1) * HEAD_DIM
+        start, stop = low // 128 * 128, -(-high // 128) * 128
+        lanes = lax.broadcasted_iota(jnp.int32, (1, stop - start), 1) + start
+        return start, stop, ((lanes >= low) & (lanes < high)).astype(f32)
+
+    def add_parts(parts, start, product):
+        for j in range(product.shape[1] // 128):
+            piece = product[:, j * 128 : (j + 1) * 128]
+            at = start // 128 + j
+            parts[at] = piece if parts[at] is None else parts[at] + piece
+
+    def no_parts():
+        return [None] * (HALF // 128)
+
+    def forward(group, between=()):
+        parts = no_parts()
+        for i in range(GROUP):
+            start, stop, mask = window(i)
+            masked = q_ref[group, :, start:stop] * mask.astype(bf16)
+            scores = dot_nt(masked, k_ref[group, :, start:stop]) * scale
+            biggest = jnp.max(scores, axis=-1, keepdims=True)
+            exponent = jnp.exp(scores - biggest)
+            softmax = exponent / jnp.sum(exponent, axis=-1, keepdims=True)
+            p_ref[group * GROUP + i] = softmax
+            add_parts(parts, start, dot_nn(softmax.astype(bf16), v_ref[group, :, start:stop]) * mask)
+            if i < len(between):
+                between[i]()
+        att_ref[:, pl.ds(group * HALF, HALF)] = jnp.concatenate(parts, axis=1).astype(bf16)
+
+    def backward(group, between=()):
+        query_parts, key_parts, value_parts = no_parts(), no_parts(), no_parts()
+        for i in range(GROUP):
+            start, stop, mask = window(i)
+            softmax = p_ref[group * GROUP + i]
+            grads = ga_ref[:, group * HALF + start : group * HALF + stop]
+            weights_grad = dot_nt(grads * mask.astype(bf16), v_ref[group, :, start:stop])
+            weighted = jnp.sum(softmax * weights_grad, axis=-1, keepdims=True)
+            grad_scores = (softmax * (weights_grad - weighted)).astype(bf16)
+            scaled = mask * scale
+            add_parts(query_parts, start, dot_nn(grad_scores, k_ref[group, :, start:stop]) * scaled)
+            add_parts(key_parts, start, dot_tn(grad_scores, q_ref[group, :, start:stop]) * scaled)
+            add_parts(value_parts, start, dot_tn(softmax.astype(bf16), grads) * mask)
+            if i < len(between):
+                between[i]()
+        gq_ref[group] = jnp.concatenate(query_parts, axis=1).astype(bf16)
+        gk_ref[group] = jnp.concatenate(key_parts, axis=1)
+        gv_ref[group] = jnp.concatenate(value_parts, axis=1)
+        for which, full in enumerate((gk_ref, gv_ref)):
+            for side in range(2):
+                rows = full[group, pl.ds(row_count + side * halo_rows, halo_rows), :]
+                grad_halo_out[group, which, side] = rows.astype(bf16)
+                grad_halo_copy(group, which, side).start()
+
+    def own_cells(group, which):
+        full = (gk_ref, gv_ref)[which]
+        for side in range(2):
+            grad_halo_copy(group, which, side).wait_recv()
+        rows = full[group, pl.ds(0, row_count), :].reshape(lat_rows, lon_cols, HALF)
+        shape = (lat_rows, MARGIN, HALF)
+        last = grad_halo_in[group, which, 0].astype(f32).reshape(shape)
+        first = grad_halo_in[group, which, 1].astype(f32).reshape(shape)
+        rows = jnp.concatenate(
+            [
+                rows[:, :MARGIN] + first,
+                rows[:, MARGIN : lon_cols - MARGIN],
+                rows[:, lon_cols - MARGIN :] + last,
+            ],
+            axis=1,
+        )
+        return rows.reshape(row_count, HALF).astype(bf16)
+
+    def add_grad_normed(group, which, first=False):
+        full = weights[qkv_chunk(group, which)]
+        if which != QUERY:
+            (k_ref, v_ref)[which][group, pl.ds(0, row_count)] = own_cells(group, which)
+
+        def step(f, _):
+            if which == QUERY:
+                rows = gq_ref[group]
+            else:
+                rows = (k_ref, v_ref)[which][group, pl.ds(0, row_count)]
+            product = dot_nt(rows, full[f].reshape(depth, HALF))
+            if first:
+                gn_ref[:, columns_of(f)] = product
+            else:
+                gn_ref[:, columns_of(f)] += product
+            return 0
+
+        lax.fori_loop(0, fsdp, step, 0)
+
+    advance((3, 4))
+    project(0, KEY)
+    advance((8, 1), (7, 2), (6, 3), (4, 4))
+    project(0, VALUE)
+    advance((5, 4))
+    project(0, QUERY)
+    advance((8, 2), (7, 3))
+    await_halos(0)
+    forward(0, (lambda: None, lambda: advance((8, 3))))
+    advance((6, 4))
+    project(1, KEY)
+    advance((7, 4))
+    project(1, VALUE)
+    backward(0)
+    advance((8, 4))
+    project(1, QUERY)
+    await_halos(1)
+    forward(1)
+    for d, half in out_parts:
+        columns = out_columns(d, half)
+        mixed = dot_nn(att_ref[...], out_block(d, half))
+        hidden_ref[:, columns] = (tokens_ref[:, columns].astype(f32) + mixed).astype(bf16)
+
+    def term_step(f, _):
+        term_ref[f] = dot_tn(rows_ref[...], hidden_ref[:, columns_of(f)]).reshape(
+            term_ref.shape[1:]
+        )
+        return 0
+
+    lax.fori_loop(0, fsdp, term_step, 0)
+
+    core_copy = remote(term_ref.at[:, 1 - core], rs0, rs_send.at[0], rs_recv.at[0], sibling)
+    y_copy = remote(snd1, rs1, rs_send.at[1], rs_recv.at[1], y_side)
+    x_copy = remote(snd2, rs2, rs_send.at[2], rs_recv.at[2], x_side)
+    z_copies = [
+        remote(
+            acc2.at[(me + k) % fsdp],
+            rs3.at[k - 1],
+            rs_send.at[5 + k],
+            rs_recv.at[5 + k],
+            {"fsdp": (me + k) % fsdp},
+        )
+        for k in range(1, fsdp)
+    ]
+    back_parts = [full_grad.at[core, ty, tx], full_grad.at[core, ty], full_grad.at[core]]
+    back = [
+        remote(part, part, rs_send.at[3 + i], rs_recv.at[3 + i], device)
+        for i, (part, device) in enumerate(zip(back_parts, (x_side, y_side, sibling)))
+    ]
+
+    def reduce_y():
+        core_copy.wait_recv()
+        theirs = term_ref[:, core, 1 - ty] + rs0[:, 1 - ty]
+        snd1[...] = theirs.reshape(snd1.shape).astype(bf16)
+        y_copy.start()
+        acc1[...] = term_ref[:, core, ty] + rs0[:, ty]
+
+    def reduce_x():
+        y_copy.wait_recv()
+        acc1[...] = acc1[...] + rs1[...].astype(f32).reshape(acc1.shape)
+        snd2[...] = acc1[:, 1 - tx]
+        x_copy.start()
+
+    def reduce_z():
+        x_copy.wait_recv()
+        acc2[...] = acc1[:, tx] + rs2[...]
+        for copy in z_copies:
+            copy.start()
+
+    core_copy.start()
+    backward(1, (lambda: None, reduce_y))
+    add_grad_normed(0, QUERY, first=True)
+    add_grad_normed(0, KEY)
+    reduce_x()
+    add_grad_normed(0, VALUE)
+    add_grad_normed(1, QUERY)
+    reduce_z()
+
+    head_out = dot_nn(hidden_ref[...], w_head_shuffled[...])
+    head_out = jnp.concatenate(
+        [
+            jnp.concatenate(
+                [
+                    head_out[i * lon_cols : (i + 1) * lon_cols, b * width : (b + 1) * width]
+                    for b in range(4)
+                ],
+                axis=0,
+            )
+            for i in range(lat_rows)
+        ],
+        axis=1,
+    )
+    shuffled_ref[...] = split_dot(dot_nn, head_out.T, to_phase) + residual_ref[...]
+    for i in range(lat_rows):
+        for a in range(4):
+            fine_ref[fine_rows(i, a), :] = shuffled_ref[cell_rows(i, a), :]
+
+    for copy in z_copies:
+        copy.wait_recv()
+    summed = acc2[me]
+    for k in range(1, fsdp):
+        summed = summed + rs3[k - 1]
+    full_grad[core, ty, tx] = summed
+    back[0].start()
+    add_grad_normed(1, KEY)
+    back[0].wait_recv()
+    back[1].start()
+    add_grad_normed(1, VALUE)
+    back[1].wait_recv()
+    back[2].start()
+
+    _, inverse_dev = normalised()
+    grad_input = norm_backward(gn_ref[...], standard_ref[...], inverse_dev, gain_ref[...])
+    grad_tokens_ref[...] = (gh_ref[...] + grad_input).astype(bf16)
+
+    back[2].wait_recv()
+    grad_head_ref[...] = full_grad[...]
+
+    for chunk in range(CHUNKS):
+        for stage in range(4):
+            for k in range(1, fsdp):
+                weight_copy(chunk, stage, k).wait_send()
+    for group in range(GROUPS):
+        for which in range(2):
+            for side in range(2):
+                halo_copy(group, which, side).wait_send()
+                grad_halo_copy(group, which, side).wait_send()
+    for copy in coarse_copies + [core_copy, y_copy, x_copy] + z_copies + back:
+        copy.wait_send()
+
+
+def fused_shards(
+    tokens, norm_gain, query_key_value_weight, out_weight, head_weight, coarse, grad_fine
+):
+    fsdp = lax.axis_size("fsdp")
+    lat_rows, lon_cols = tokens.shape[1:3]
+    row_count = lat_rows * lon_cols
+    halo_rows = lat_rows * MARGIN
+    key_count = row_count + 2 * halo_rows
+    depth, qkv_width = query_key_value_weight.shape
+    piece = depth // 8
+    out_piece = out_weight.shape[0] // 4
+    head_piece = HEAD_OUT // 8
+    bf16, f32 = jnp.bfloat16, jnp.float32
+    vmem = pl.BlockSpec(memory_space=pltpu.VMEM)
+    hbm = pl.BlockSpec(memory_space=pl.ANY)
+    coarse_rows = jnp.pad(
+        coarse[0].transpose(2, 1, 0), ((0, 0), (0, 0), (0, PADDED - VARS))
+    ).reshape(lon_cols, lat_rows * PADDED)
+
+    def full(rows, columns):
+        return pltpu.VMEM((fsdp, 2, 2, 2, rows, columns), bf16)
+
+    fine_rows = VARS * 4 * lat_rows
+    shuffled = 4 * lat_rows * PADDED
+    fine_grid, grad_tokens, grad_head = pl.pallas_call(
+        functools.partial(block_kernel, fsdp, lat_rows, lon_cols),
+        out_shape=(
+            jax.ShapeDtypeStruct((fine_rows, 4 * lon_cols), f32),
+            jax.ShapeDtypeStruct((row_count, D), bf16),
+            jax.ShapeDtypeStruct((2, 2, 2, head_piece, depth), f32),
+        ),
+        in_specs=[vmem, vmem, hbm, hbm, vmem, vmem, vmem],
+        out_specs=(vmem, vmem, vmem),
+        scratch_shapes=[
+            full(out_piece, HALF),
+            full(out_piece, HALF),
+            full(piece, HEAD_OUT),
+        ]
+        + [full(piece, HALF)] * 6
+        + [
+            pltpu.VMEM((row_count, D), f32),
+            pltpu.VMEM((row_count, D), bf16),
+            pltpu.VMEM((GROUPS, row_count, HALF), bf16),
+            pltpu.VMEM((GROUPS, key_count, HALF), bf16),
+            pltpu.VMEM((GROUPS, key_count, HALF), bf16),
+            pltpu.VMEM((HEADS, row_count, key_count), f32),
+            pltpu.VMEM((row_count, INNER), bf16),
+            pltpu.VMEM((row_count, INNER), bf16),
+            pltpu.VMEM((row_count, D), f32),
+            pltpu.VMEM((row_count, D), bf16),
+            pltpu.VMEM((GROUPS, row_count, HALF), bf16),
+            pltpu.VMEM((GROUPS, key_count, HALF), f32),
+            pltpu.VMEM((GROUPS, key_count, HALF), f32),
+            pltpu.VMEM((row_count, D), f32),
+            pltpu.VMEM((row_count, HEAD_OUT), bf16),
+            pltpu.VMEM((shuffled, 4 * lon_cols), f32),
+            pltpu.VMEM((shuffled, 4 * lon_cols), f32),
+            pltpu.VMEM((lon_cols + 2 * MARGIN, lat_rows * PADDED), f32),
+            pltpu.VMEM((D, 16 * PADDED), bf16),
+            pltpu.VMEM((GROUPS, 2, 2, halo_rows, HALF), bf16),
+            pltpu.VMEM((GROUPS, 2, 2, halo_rows, HALF), bf16),
+            pltpu.VMEM((GROUPS, 2, 2, halo_rows, HALF), bf16),
+            pltpu.VMEM((fsdp, 2, 2, 2, head_piece, depth), f32),
+            pltpu.VMEM((fsdp, 2, 2, head_piece, depth), f32),
+            pltpu.VMEM((fsdp, 2 * head_piece, depth), bf16),
+            pltpu.VMEM((fsdp, 2 * head_piece, depth), bf16),
+            pltpu.VMEM((fsdp, 2, head_piece, depth), f32),
+            pltpu.VMEM((fsdp, head_piece, depth), f32),
+            pltpu.VMEM((fsdp, head_piece, depth), f32),
+            pltpu.VMEM((fsdp, head_piece, depth), f32),
+            pltpu.VMEM((fsdp - 1, head_piece, depth), f32),
+            pltpu.VMEM((2, 2, 2, head_piece, depth), f32),
+            pltpu.SemaphoreType.DMA((10,)),
+            pltpu.SemaphoreType.DMA((CHUNKS, 4, fsdp - 1)),
+            pltpu.SemaphoreType.DMA((CHUNKS, 4, fsdp - 1)),
+            pltpu.SemaphoreType.DMA((2, GROUPS, 2, 2)),
+            pltpu.SemaphoreType.DMA((2, GROUPS, 2, 2)),
+            pltpu.SemaphoreType.DMA((2,)),
+            pltpu.SemaphoreType.DMA((2,)),
+            pltpu.SemaphoreType.DMA((5 + fsdp,)),
+            pltpu.SemaphoreType.DMA((5 + fsdp,)),
+        ],
+        compiler_params=pltpu.CompilerParams(
+            collective_id=0, has_side_effects=True, vmem_limit_bytes=58 * 1024 * 1024
+        ),
+        cost_estimate=pl.CostEstimate(
+            flops=int(7e9), bytes_accessed=int(1e7), transcendentals=row_count * key_count * HEADS
+        ),
+    )(
+        tokens.reshape(row_count, D),
+        norm_gain.reshape(1, D),
+        query_key_value_weight.reshape(2, 2, 2, piece, qkv_width),
+        out_weight.reshape(2, 2, out_piece, D),
+        head_weight.T,
+        coarse_rows,
+        grad_fine.reshape(fine_rows, 4 * lon_cols),
+    )
+    return (
+        fine_grid.reshape(grad_fine.shape),
+        grad_tokens.reshape(tokens.shape),
+        grad_head.reshape(HEAD_OUT, depth).T,
+    )
+
+
+def fits_pieces(tokens, qkv, out_weight):
+    if lax.axis_size("dp") != 2 or lax.axis_size("tile") != 4 or lax.axis_size("fsdp") < 2:
+        return False
+    lat_rows, lon_cols = tokens.shape[1:3]
+    if lat_rows % 2 or 4 * lon_cols != 128 or VARS > PADDED or 16 * VARS != HEAD_OUT:
+        return False
+    return qkv.shape[0] % 128 == 0 and out_weight.shape[0] % 64 == 0
+
+
+def any_shards(*arguments):
+    if fits_pieces(arguments[0], arguments[2], arguments[3]):
+        return fused_shards(*arguments)
+    return shards(*arguments)
 
 
 def shards(tokens, norm_gain, query_key_value_weight, out_weight, head_weight, coarse, grad_fine):
@@ -210,7 +935,7 @@
         P(("dp", "fsdp"), None, None, "tile"),
     )
     return jax.shard_map(
-        shards,
+        any_shards,
         mesh=mesh,
         in_specs=placed,
         out_specs=(

time: 353 us -> 114 us (0.32)
  waiting for transfers between devices: 202 us -> 0 us
  Pallas kernels: 0 us -> 105 us
  matrix products: 38.3 us -> 0 us
  blocking collectives: 35.7 us -> 0 us
  local copies, waits for them, and re-layouts: 40.8 us -> 7.65 us
  between operations: 14.1 us -> 0.66 us
  other arithmetic: 12.1 us -> 0 us
  starting transfers between devices: 9.31 us -> 0 us
    all_gather x2 -> x0, waiting for transfers between devices: 137 us -> none  [the longest x1 95.1 us: shards(): lax.all_gather(query_key_value_weight, 'fsdp', axis=0, tiled=True)]
    pallas_call x0 -> x1, Pallas kernels: none -> 105 us  [fused_shards(): pl.pallas_call(functools.partial(block_kernel, fsdp, lat_rows, lon_cols),...]
    psum x1 -> x0, waiting for transfers between devices: 49.3 us -> none  [shards(): grad_head = lax.psum(head_block, ('dp', 'tile'))]
    all_gather x1 -> x0, blocking collectives: 35.7 us -> none  [shards(): full_head = lax.all_gather(head_weight, 'fsdp', axis=0, tiled=True)]
    dot_general x14 -> x0, matrix products: 34.2 us -> none  [the longest x3 10 us: contract_last(): lax.dot_general(left_side, right_side, (((1,), (1,)), ((), ())), preferre...]
    ppermute x6 -> x0, waiting for transfers between devices: 15.2 us -> none  [the longest x2 15.2 us: from_behind(): return lax.ppermute(value, axis, pairs)]
    convert_element_type x5 -> x0, other arithmetic: 9.05 us -> none  [the longest x1 3.27 us: attend_backward(): grad_scores = (softmax_out * (grad_weights - weighted)).astype(jnp.bfloat16)]
    ppermute x6 -> x0, starting transfers between devices: 8.97 us -> none  [the longest x2 6.53 us: with_halo(): after = lax.ppermute(leading, axis, down)]
  transfers between devices with their start and end apart: 10 -> 0, of which waited for: 5 -> 0; matrix products, arithmetic and copies ran while one was open for 16% -> 0% of each run, Pallas kernels for 0% -> 0%
where the time goes in v2:
time: 114 us
  Pallas kernels  105 us (92%)
  local copies, waits for them, and re-layouts  7.65 us (7%)
    pallas_call x1, Pallas kernels, fused_shards(): pl.pallas_call(functools.partial(block_kernel, fsdp, lat_rows, lon_cols),...  105 us
    unnamed x6, local copies, waits for them, and re-layouts  5.63 us

profile of v2, /device:TPU:0, one launch (start us, length us, event | category | flops | bytes accessed | tf_op | source)
XLA Modules:
  0.0 113.5 jit_solution(17037237150566841054)
XLA Ops:
  0.6 1.3 %reshape.34.gain_ref = f32[1,1536]{1,0:T(1,128)} reshape(f32[1536]{0:T(1024)} %param.8) | data formatting | bytes 12288 | tf_op jit(solution)/shard_map/reshape | solution.py:823
  1.9 1.0 copy.11
  3.0 0.7 reshape.37.coarse_ref
  3.7 105.2 %shard_map.94 = (f32[640,128]{1,0:T(8,128)}, bf16[256,1536]{1,0:T(8,128)(2,1)}, f32[2,2,2,40,384]{4,3,2,1,0:T(8,128)}) custom-call(bf16[256,1536]{1,0:T(8,128)(2,1)} %bitcast.18, f32[1,1536]{1,0:T(1,128)} %reshape.34.gain_ref, bf16[2,2,2,48,2304]{4,3,2,1,0:T(8,128)(2,1)} %bitcast.17, bf16[2,2,48,1536]{3,2,1,0:T(8,128)(2,1)} %bitcast.19, ...), custom_call_target="tpu_custom_call" | custom-call | flops 7000000000 | bytes 10000000 | tf_op jit(solution)/shard_map/pallas_call | solution.py:757
  108.9 0.0 copy-start
  108.9 1.8 %copy.15 = f32[1,20,32,128]{3,2,1,0:T(8,128)} copy(f32[1,20,32,128]{3,2,1,0:T(8,128)} %bitcast.15) | data formatting | bytes 655360
  110.7 2.1 %copy.16 = bf16[1,8,32,1536]{3,2,1,0:T(8,128)(2,1)} copy(bf16[1,8,32,1536]{3,2,1,0:T(8,128)(2,1)} %bitcast.13) | data formatting | bytes 1572864
  112.7 0.0 copy-done
  112.7 0.8 copy.17
  (1 shorter events, 0.0 us)
Async XLA Ops:
  108.9 3.8 %copy-start = (f32[2,2,2,40,384]{4,3,2,1,0:T(8,128)S(1)}, f32[2,2,2,40,384]{4,3,2,1,0:T(8,128)}, u32[]{:S(2)}) copy-start(f32[2,2,2,40,384]{4,3,2,1,0:T(8,128)} %get-tuple-element.8) | copy-start | bytes 1474564

commit v3 on v2

--- a/solution.py
+++ b/solution.py
@@ -152,6 +152,7 @@
 GROUPS = 2
 GROUP = HEADS // GROUPS
 PADDED = 32
+WINDOW = 3
 
 
 def split_dot(dot, left_side, right_side):
@@ -232,6 +233,8 @@
     coarse_recv,
     rs_send,
     rs_recv,
+    back_send,
+    back_recv,
 ):
     row_count = lat_rows * lon_cols
     halo_rows = lat_rows * MARGIN
@@ -301,6 +304,8 @@
                     weight_copy(chunk, stage - 1, k).wait_recv()
                 if stage < 4:
                     weight_copy(chunk, stage, k).start()
+            if stage == 1 and chunk + WINDOW < CHUNKS:
+                advance((chunk + WINDOW, 0))
 
     def local_copies():
         pairs = []
@@ -317,8 +322,6 @@
     copies = local_copies()
     for copy in copies:
         copy.start()
-    eye = spread(depth, depth, lambda r, c: (r == c).astype(f32)).astype(bf16)
-    w_head[me] = dot_nt(eye, head_ref[...]).astype(bf16).reshape(w_head.shape[1:])
     coarse_pad[pl.ds(MARGIN, lon_cols), :] = coarse_ref[...]
 
     barrier = pltpu.get_barrier_semaphore()
@@ -329,7 +332,10 @@
         pl.semaphore_signal(barrier, inc=1, device_id=partner, device_id_type=pl.DeviceIdType.MESH)
     pl.semaphore_wait(barrier, len(partners))
 
-    advance(*[(chunk, 0) for chunk in range(CHUNKS)])
+    advance((OUT0, 0), (OUT1, 0))
+    eye = spread(depth, depth, lambda r, c: (r == c).astype(f32)).astype(bf16)
+    w_head[me] = dot_nt(eye, head_ref[...]).astype(bf16).reshape(w_head.shape[1:])
+    advance((HEAD, 0))
     coarse_copies = [
         remote(
             coarse_pad.at[pl.ds(lon_cols, MARGIN)],
@@ -358,7 +364,7 @@
     standard_ref[...] = standard
     normed_ref[...] = (standard * gain_ref[...]).astype(bf16)
 
-    advance((OUT0, 1), (OUT1, 1), (HEAD, 1))
+    advance((0, 1))
 
     def cell_rows(i, a):
         return pl.ds((i * 4 + a) * PADDED, VARS)
@@ -400,45 +406,9 @@
     )
     rows_ref[...] = dot_nn(turned.astype(bf16), to_feature).astype(bf16)
 
-    advance((OUT0, 2), (OUT1, 2), (HEAD, 2))
-    advance((3, 1), (4, 1))
-    advance((OUT0, 3), (OUT1, 3), (HEAD, 3))
-    advance((5, 1), (3, 2), (4, 2))
+    advance((1, 1), (0, 2), (2, 1), (1, 2), (0, 3), (3, 1), (2, 2))
     for copy in copies:
         copy.wait()
-
-    def columns_of(f):
-        return pl.ds(pl.multiple_of(f * depth, 128), depth)
-
-    advance((HEAD, 4))
-
-    def grad_hidden_step(f, _):
-        rows = w_head[f].reshape(depth, HEAD_OUT)
-        gh_ref[:, columns_of(f)] = dot_nt(rows_ref[...], rows)
-        w_head_shuffled[pl.ds(pl.multiple_of(f * depth, 128), depth), :] = dot_nt(
-            rows, to_feature
-        ).astype(bf16)
-        return 0
-
-    lax.fori_loop(0, fsdp, grad_hidden_step, 0)
-    advance((6, 1), (5, 2), (3, 3), (4, 3))
-    advance((OUT0, 4), (OUT1, 4))
-    out_parts = [(d, half) for d in range(2) for half in range(2)]
-
-    def out_block(d, half):
-        full = (w_out0, w_out1)[half]
-        return full[:, d].reshape(INNER, HALF)
-
-    def out_columns(d, half):
-        return pl.ds(d * 2 * HALF + half * HALF, HALF)
-
-    grad_attended = jnp.zeros((row_count, INNER), f32)
-    for d, half in out_parts:
-        low = gh_ref[:, out_columns(d, half)].astype(bf16)
-        grad_attended = grad_attended + dot_nt(low, out_block(d, half))
-    ga_ref[...] = grad_attended.astype(bf16)
-
-    advance((7, 1), (6, 2), (5, 3))
 
     for copy in coarse_copies:
         copy.wait_recv()
@@ -465,6 +435,40 @@
             residual_ref[pl.ds((i * 4 + a) * PADDED, PADDED), :] = (
                 lower * (1.0 - upper_weight) + upper * upper_weight
             )
+
+    advance((0, 4), (1, 3), (4, 1), (3, 2), (1, 4), (2, 3), (5, 1), (4, 2))
+
+    def columns_of(f):
+        return pl.ds(pl.multiple_of(f * depth, 128), depth)
+
+    advance((2, 4))
+
+    def grad_hidden_step(f, _):
+        rows = w_head[f].reshape(depth, HEAD_OUT)
+        gh_ref[:, columns_of(f)] = dot_nt(rows_ref[...], rows)
+        w_head_shuffled[pl.ds(pl.multiple_of(f * depth, 128), depth), :] = dot_nt(
+            rows, to_feature
+        ).astype(bf16)
+        return 0
+
+    lax.fori_loop(0, fsdp, grad_hidden_step, 0)
+    advance((3, 3), (6, 1), (5, 2))
+    out_parts = [(d, half) for d in range(2) for half in range(2)]
+
+    def out_block(d, half):
+        full = (w_out0, w_out1)[half]
+        return full[:, d].reshape(INNER, HALF)
+
+    def out_columns(d, half):
+        return pl.ds(d * 2 * HALF + half * HALF, HALF)
+
+    grad_attended = jnp.zeros((row_count, INNER), f32)
+    for d, half in out_parts:
+        low = gh_ref[:, out_columns(d, half)].astype(bf16)
+        grad_attended = grad_attended + dot_nt(low, out_block(d, half))
+    ga_ref[...] = grad_attended.astype(bf16)
+
+    advance((4, 3), (7, 1), (6, 2))
 
     def edge(rows, first):
         shaped = rows.reshape(lat_rows, lon_cols, rows.shape[-1])
@@ -601,20 +605,27 @@
 
     advance((3, 4))
     project(0, KEY)
-    advance((8, 1), (7, 2), (6, 3), (4, 4))
+    advance((4, 4))
     project(0, VALUE)
-    advance((5, 4))
+    advance((5, 3), (8, 1), (7, 2), (5, 4))
     project(0, QUERY)
-    advance((8, 2), (7, 3))
+    advance((6, 3))
     await_halos(0)
-    forward(0, (lambda: None, lambda: advance((8, 3))))
+    forward(0, (lambda: None, lambda: advance((8, 2)), lambda: advance((7, 3))))
     advance((6, 4))
     project(1, KEY)
-    advance((7, 4))
-    project(1, VALUE)
-    backward(0)
+
+    def next_values():
+        advance((7, 4))
+        project(1, VALUE)
+
+    backward(0, (lambda: advance((8, 3)), next_values))
     advance((8, 4))
     project(1, QUERY)
+    for chunk in range(CHUNKS):
+        for stage in range(4):
+            for k in range(1, fsdp):
+                weight_copy(chunk, stage, k).wait_send()
     await_halos(1)
     forward(1)
     for d, half in out_parts:
@@ -643,11 +654,20 @@
         )
         for k in range(1, fsdp)
     ]
-    back_parts = [full_grad.at[core, ty, tx], full_grad.at[core, ty], full_grad.at[core]]
+    mine = full_grad.at[core, ty, tx]
     back = [
-        remote(part, part, rs_send.at[3 + i], rs_recv.at[3 + i], device)
-        for i, (part, device) in enumerate(zip(back_parts, (x_side, y_side, sibling)))
+        remote(
+            mine,
+            mine,
+            back_send.at[i - 1],
+            back_recv.at[i - 1],
+            {"tile": (tile + i) % tiles},
+        )
+        for i in range(1, 4)
     ]
+    last_back = remote(
+        full_grad.at[core], full_grad.at[core], rs_send.at[3], rs_recv.at[3], sibling
+    )
 
     def reduce_y():
         core_copy.wait_recv()
@@ -702,31 +722,27 @@
     for k in range(1, fsdp):
         summed = summed + rs3[k - 1]
     full_grad[core, ty, tx] = summed
-    back[0].start()
+    for copy in back:
+        copy.start()
     add_grad_normed(1, KEY)
-    back[0].wait_recv()
-    back[1].start()
     add_grad_normed(1, VALUE)
-    back[1].wait_recv()
-    back[2].start()
+    for copy in back:
+        copy.wait_recv()
+    last_back.start()
 
     _, inverse_dev = normalised()
     grad_input = norm_backward(gn_ref[...], standard_ref[...], inverse_dev, gain_ref[...])
     grad_tokens_ref[...] = (gh_ref[...] + grad_input).astype(bf16)
 
-    back[2].wait_recv()
+    last_back.wait_recv()
     grad_head_ref[...] = full_grad[...]
 
-    for chunk in range(CHUNKS):
-        for stage in range(4):
-            for k in range(1, fsdp):
-                weight_copy(chunk, stage, k).wait_send()
     for group in range(GROUPS):
         for which in range(2):
             for side in range(2):
                 halo_copy(group, which, side).wait_send()
                 grad_halo_copy(group, which, side).wait_send()
-    for copy in coarse_copies + [core_copy, y_copy, x_copy] + z_copies + back:
+    for copy in coarse_copies + [core_copy, y_copy, x_copy, last_back] + z_copies + back:
         copy.wait_send()
 
 
@@ -811,6 +827,8 @@
             pltpu.SemaphoreType.DMA((2,)),
             pltpu.SemaphoreType.DMA((5 + fsdp,)),
             pltpu.SemaphoreType.DMA((5 + fsdp,)),
+            pltpu.SemaphoreType.DMA((3,)),
+            pltpu.SemaphoreType.DMA((3,)),
         ],
         compiler_params=pltpu.CompilerParams(
             collective_id=0, has_side_effects=True, vmem_limit_bytes=58 * 1024 * 1024

time: 114 us -> 108 us (0.947)
  Pallas kernels: 105 us -> 99.4 us
    pallas_call x1, Pallas kernels: 105 us -> 99.4 us  [fused_shards(): pl.pallas_call(functools.partial(block_kernel, fsdp, lat_rows, lon_cols),...]
where the time goes in v3:
time: 108 us
  Pallas kernels  99.4 us (92%)
  local copies, waits for them, and re-layouts  7.65 us (7%)
    pallas_call x1, Pallas kernels, fused_shards(): pl.pallas_call(functools.partial(block_kernel, fsdp, lat_rows, lon_cols),...  99.4 us
    unnamed x6, local copies, waits for them, and re-layouts  5.63 us

profile of v3, /device:TPU:0, one launch (start us, length us, event | category | flops | bytes accessed | tf_op | source)
XLA Modules:
  0.0 107.8 jit_solution(12877325017893782897)
XLA Ops:
  0.6 1.3 %reshape.34.gain_ref = f32[1,1536]{1,0:T(1,128)} reshape(f32[1536]{0:T(1024)} %param.8) | data formatting | bytes 12288 | tf_op jit(solution)/shard_map/reshape | solution.py:841
  1.9 1.0 copy.11
  3.0 0.7 reshape.37.coarse_ref
  3.7 99.4 %shard_map.94 = (f32[640,128]{1,0:T(8,128)}, bf16[256,1536]{1,0:T(8,128)(2,1)}, f32[2,2,2,40,384]{4,3,2,1,0:T(8,128)}) custom-call(bf16[256,1536]{1,0:T(8,128)(2,1)} %bitcast.18, f32[1,1536]{1,0:T(1,128)} %reshape.34.gain_ref, bf16[2,2,2,48,2304]{4,3,2,1,0:T(8,128)(2,1)} %bitcast.17, bf16[2,2,48,1536]{3,2,1,0:T(8,128)(2,1)} %bitcast.19, ...), custom_call_target="tpu_custom_call" | custom-call | flops 7000000000 | bytes 10000000 | tf_op jit(solution)/shard_map/pallas_call | solution.py:773
  103.1 0.0 copy-start
  103.1 1.8 %copy.15 = f32[1,20,32,128]{3,2,1,0:T(8,128)} copy(f32[1,20,32,128]{3,2,1,0:T(8,128)} %bitcast.15) | data formatting | bytes 655360
  104.9 2.1 %copy.16 = bf16[1,8,32,1536]{3,2,1,0:T(8,128)(2,1)} copy(bf16[1,8,32,1536]{3,2,1,0:T(8,128)(2,1)} %bitcast.13) | data formatting | bytes 1572864
  107.0 0.0 copy-done
  107.0 0.8 copy.17
  (1 shorter events, 0.0 us)
Async XLA Ops:
  103.1 3.8 %copy-start = (f32[2,2,2,40,384]{4,3,2,1,0:T(8,128)S(1)}, f32[2,2,2,40,384]{4,3,2,1,0:T(8,128)}, u32[]{:S(2)}) copy-start(f32[2,2,2,40,384]{4,3,2,1,0:T(8,128)} %get-tuple-element.8) | copy-start | bytes 1474564

commit v4 on v3

--- a/solution.py
+++ b/solution.py
@@ -193,6 +193,7 @@
     w_value1,
     w_query1,
     standard_ref,
+    inverse_ref,
     normed_ref,
     q_ref,
     k_ref,
@@ -322,7 +323,6 @@
     copies = local_copies()
     for copy in copies:
         copy.start()
-    coarse_pad[pl.ds(MARGIN, lon_cols), :] = coarse_ref[...]
 
     barrier = pltpu.get_barrier_semaphore()
     partners = [{"tile": (tile + i) % tiles} for i in range(1, 4)]
@@ -336,6 +336,15 @@
     eye = spread(depth, depth, lambda r, c: (r == c).astype(f32)).astype(bf16)
     w_head[me] = dot_nt(eye, head_ref[...]).astype(bf16).reshape(w_head.shape[1:])
     advance((HEAD, 0))
+    cells = lat_rows * PADDED
+    shuffled_ref[pl.ds(0, cells), :] = jnp.zeros((cells, fine_cols), f32)
+    shuffled_ref[pl.ds(0, VARS * lat_rows), pl.ds(0, lon_cols)] = coarse_ref[...]
+    by_latitude = spread(
+        cells, cells, lambda r, c: (c == (r % lat_rows) * PADDED + r // lat_rows).astype(f32)
+    ).astype(bf16)
+    coarse_pad[pl.ds(MARGIN, lon_cols), :] = split_dot(
+        dot_nn, shuffled_ref[pl.ds(0, cells), :].T[:lon_cols], by_latitude
+    )
     coarse_copies = [
         remote(
             coarse_pad.at[pl.ds(lon_cols, MARGIN)],
@@ -360,9 +369,10 @@
     def normalised():
         return layer_norm(tokens_ref[...].astype(f32))
 
-    standard, _ = normalised()
+    standard, inverse_dev = normalised()
     standard_ref[...] = standard
-    normed_ref[...] = (standard * gain_ref[...]).astype(bf16)
+    inverse_ref[...] = inverse_dev
+    normed_ref[...] = (standard * gain_ref[...][None, :]).astype(bf16)
 
     advance((0, 1))
 
@@ -642,8 +652,22 @@
     lax.fori_loop(0, fsdp, term_step, 0)
 
     core_copy = remote(term_ref.at[:, 1 - core], rs0, rs_send.at[0], rs_recv.at[0], sibling)
-    y_copy = remote(snd1, rs1, rs_send.at[1], rs_recv.at[1], y_side)
-    x_copy = remote(snd2, rs2, rs_send.at[2], rs_recv.at[2], x_side)
+    half = fsdp // 2
+    routes = (
+        (pl.ds(0, half), ty, tx, y_side, x_side),
+        (pl.ds(half, fsdp - half), tx, ty, x_side, y_side),
+    )
+    first_copies = [
+        remote(snd1.at[part], rs1.at[part], rs_send.at[1 + i], rs_recv.at[1 + i], near)
+        for i, (part, _, _, near, _) in enumerate(routes)
+    ]
+    second_copies = [
+        remote(snd2.at[part], rs2.at[part], rs_send.at[3 + i], rs_recv.at[3 + i], far)
+        for i, (part, _, _, _, far) in enumerate(routes)
+    ]
+    on_second = me // half
+    outer = ty + on_second * (tx - ty)
+    inner = tx + on_second * (ty - tx)
     z_copies = [
         remote(
             acc2.at[(me + k) % fsdp],
@@ -654,7 +678,7 @@
         )
         for k in range(1, fsdp)
     ]
-    mine = full_grad.at[core, ty, tx]
+    mine = full_grad.at[core, outer, inner]
     back = [
         remote(
             mine,
@@ -666,33 +690,39 @@
         for i in range(1, 4)
     ]
     last_back = remote(
-        full_grad.at[core], full_grad.at[core], rs_send.at[3], rs_recv.at[3], sibling
-    )
-
-    def reduce_y():
+        full_grad.at[core], full_grad.at[core], rs_send.at[5], rs_recv.at[5], sibling
+    )
+
+    def reduce_first():
         core_copy.wait_recv()
-        theirs = term_ref[:, core, 1 - ty] + rs0[:, 1 - ty]
-        snd1[...] = theirs.reshape(snd1.shape).astype(bf16)
-        y_copy.start()
-        acc1[...] = term_ref[:, core, ty] + rs0[:, ty]
-
-    def reduce_x():
-        y_copy.wait_recv()
-        acc1[...] = acc1[...] + rs1[...].astype(f32).reshape(acc1.shape)
-        snd2[...] = acc1[:, 1 - tx]
-        x_copy.start()
+        for copy, (part, first, _, _, _) in zip(first_copies, routes):
+            theirs = term_ref[part, core, 1 - first] + rs0[part, 1 - first]
+            snd1[part] = theirs.reshape(-1, *snd1.shape[1:]).astype(bf16)
+            copy.start()
+        for part, first, _, _, _ in routes:
+            acc1[part] = term_ref[part, core, first] + rs0[part, first]
+
+    def reduce_second():
+        for copy, (part, _, second, _, _) in zip(first_copies, routes):
+            copy.wait_recv()
+            arrived = rs1[part].astype(f32)
+            acc1[part] = acc1[part] + arrived.reshape(-1, *acc1.shape[1:])
+        for copy, (part, _, second, _, _) in zip(second_copies, routes):
+            snd2[part] = acc1[part, 1 - second]
+            copy.start()
 
     def reduce_z():
-        x_copy.wait_recv()
-        acc2[...] = acc1[:, tx] + rs2[...]
+        for copy, (part, _, second, _, _) in zip(second_copies, routes):
+            copy.wait_recv()
+            acc2[part] = acc1[part, second] + rs2[part]
         for copy in z_copies:
             copy.start()
 
     core_copy.start()
-    backward(1, (lambda: None, reduce_y))
+    backward(1, (lambda: None, reduce_first))
     add_grad_normed(0, QUERY, first=True)
     add_grad_normed(0, KEY)
-    reduce_x()
+    reduce_second()
     add_grad_normed(0, VALUE)
     add_grad_normed(1, QUERY)
     reduce_z()
@@ -721,7 +751,7 @@
     summed = acc2[me]
     for k in range(1, fsdp):
         summed = summed + rs3[k - 1]
-    full_grad[core, ty, tx] = summed
+    full_grad[core, outer, inner] = summed
     for copy in back:
         copy.start()
     add_grad_normed(1, KEY)
@@ -730,8 +760,9 @@
         copy.wait_recv()
     last_back.start()
 
-    _, inverse_dev = normalised()
-    grad_input = norm_backward(gn_ref[...], standard_ref[...], inverse_dev, gain_ref[...])
+    grad_input = norm_backward(
+        gn_ref[...], standard_ref[...], inverse_ref[...], gain_ref[...][None, :]
+    )
     grad_tokens_ref[...] = (gh_ref[...] + grad_input).astype(bf16)
 
     last_back.wait_recv()
@@ -742,7 +773,7 @@
             for side in range(2):
                 halo_copy(group, which, side).wait_send()
                 grad_halo_copy(group, which, side).wait_send()
-    for copy in coarse_copies + [core_copy, y_copy, x_copy, last_back] + z_copies + back:
+    for copy in coarse_copies + [core_copy, last_back] + first_copies + second_copies + z_copies + back:
         copy.wait_send()
 
 
@@ -761,10 +792,6 @@
     bf16, f32 = jnp.bfloat16, jnp.float32
     vmem = pl.BlockSpec(memory_space=pltpu.VMEM)
     hbm = pl.BlockSpec(memory_space=pl.ANY)
-    coarse_rows = jnp.pad(
-        coarse[0].transpose(2, 1, 0), ((0, 0), (0, 0), (0, PADDED - VARS))
-    ).reshape(lon_cols, lat_rows * PADDED)
-
     def full(rows, columns):
         return pltpu.VMEM((fsdp, 2, 2, 2, rows, columns), bf16)
 
@@ -787,6 +814,7 @@
         + [full(piece, HALF)] * 6
         + [
             pltpu.VMEM((row_count, D), f32),
+            pltpu.VMEM((row_count, 1), f32),
             pltpu.VMEM((row_count, D), bf16),
             pltpu.VMEM((GROUPS, row_count, HALF), bf16),
             pltpu.VMEM((GROUPS, key_count, HALF), bf16),
@@ -838,11 +866,11 @@
         ),
     )(
         tokens.reshape(row_count, D),
-        norm_gain.reshape(1, D),
+        norm_gain,
         query_key_value_weight.reshape(2, 2, 2, piece, qkv_width),
         out_weight.reshape(2, 2, out_piece, D),
         head_weight.T,
-        coarse_rows,
+        coarse.reshape(VARS * lat_rows, lon_cols),
         grad_fine.reshape(fine_rows, 4 * lon_cols),
     )
     return (
@@ -853,7 +881,7 @@
 
 
 def fits_pieces(tokens, qkv, out_weight):
-    if lax.axis_size("dp") != 2 or lax.axis_size("tile") != 4 or lax.axis_size("fsdp") < 2:
+    if lax.axis_size("dp") != 2 or lax.axis_size("tile") != 4 or lax.axis_size("fsdp") % 2:
         return False
     lat_rows, lon_cols = tokens.shape[1:3]
     if lat_rows % 2 or 4 * lon_cols != 128 or VARS > PADDED or 16 * VARS != HEAD_OUT:

time: 108 us -> 100 us (0.926)
  Pallas kernels: 99.4 us -> 94.7 us
  local copies, waits for them, and re-layouts: 7.65 us -> 4.62 us
    pallas_call x1, Pallas kernels: 99.4 us -> 94.7 us  [fused_shards(): pl.pallas_call(functools.partial(block_kernel, fsdp, lat_rows, lon_cols),...]
    reshape x2 -> x0, local copies, waits for them, and re-layouts: 2.01 us -> none  [the longest x1 1.3 us: fused_shards(): norm_gain.reshape(1, D)]
    unnamed x6 -> x5, local copies, waits for them, and re-layouts: 5.63 us -> 4.62 us
where the time goes in v4:
time: 100 us; the launch traced here: 99.9 us
  Pallas kernels  94.7 us (95%)
  local copies, waits for them, and re-layouts  4.62 us (5%)
    pallas_call x1, Pallas kernels, fused_shards(): pl.pallas_call(functools.partial(block_kernel, fsdp, lat_rows, lon_cols),...  94.7 us
    unnamed x5, local copies, waits for them, and re-layouts  4.62 us

profile of v4, /device:TPU:0, one launch (start us, length us, event | category | flops | bytes accessed | tf_op | source)
XLA Modules:
  0.0 99.9 jit_solution(10149928327402199871)
XLA Ops:
  0.6 94.7 %shard_map.94 = (f32[640,128]{1,0:T(8,128)}, bf16[256,1536]{1,0:T(8,128)(2,1)}, f32[2,2,2,40,384]{4,3,2,1,0:T(8,128)}) custom-call(bf16[256,1536]{1,0:T(8,128)(2,1)} %bitcast.15, f32[1536]{0:T(1024)} %gain_ref.1, bf16[2,2,2,48,2304]{4,3,2,1,0:T(8,128)(2,1)} %bitcast.14, bf16[2,2,48,1536]{3,2,1,0:T(8,128)(2,1)} %bitcast.16, bf16[320,384]{1,0:T(8,128)(2,1)} %bitcast.18, ...), custom_call_target="tpu_custom_call" | custom-call | flops 7000000000 | bytes 10000000 | tf_op jit(solution)/shard_map/pallas_call | solution.py:800
  95.3 0.0 copy-start
  95.3 1.8 %copy.13 = f32[1,20,32,128]{3,2,1,0:T(8,128)} copy(f32[1,20,32,128]{3,2,1,0:T(8,128)} %bitcast.13) | data formatting | bytes 655360
  97.1 2.1 %copy.14 = bf16[1,8,32,1536]{3,2,1,0:T(8,128)(2,1)} copy(bf16[1,8,32,1536]{3,2,1,0:T(8,128)(2,1)} %bitcast.11) | data formatting | bytes 1572864
  99.2 0.0 copy-done
  99.2 0.8 copy.15
Async XLA Ops:
  95.3 3.8 %copy-start = (f32[2,2,2,40,384]{4,3,2,1,0:T(8,128)S(1)}, f32[2,2,2,40,384]{4,3,2,1,0:T(8,128)}, u32[]{:S(2)}) copy-start(f32[2,2,2,40,384]{4,3,2,1,0:T(8,128)} %get-tuple-element.8) | copy-start | bytes 1474564

commit v5 on v4

--- a/solution.py
+++ b/solution.py
@@ -194,6 +194,7 @@
     w_query1,
     standard_ref,
     inverse_ref,
+    mixed_ref,
     normed_ref,
     q_ref,
     k_ref,
@@ -630,6 +631,11 @@
         project(1, VALUE)
 
     backward(0, (lambda: advance((8, 3)), next_values))
+    for d, half in out_parts:
+        columns = out_columns(d, half)
+        mixed = dot_nn(att_ref[:, pl.ds(0, HALF)], out_block(d, half)[:HALF])
+        mixed_ref[:, columns] = tokens_ref[:, columns].astype(f32) + mixed
+    add_grad_normed(0, QUERY, first=True)
     advance((8, 4))
     project(1, QUERY)
     for chunk in range(CHUNKS):
@@ -640,8 +646,8 @@
     forward(1)
     for d, half in out_parts:
         columns = out_columns(d, half)
-        mixed = dot_nn(att_ref[...], out_block(d, half))
-        hidden_ref[:, columns] = (tokens_ref[:, columns].astype(f32) + mixed).astype(bf16)
+        mixed = dot_nn(att_ref[:, pl.ds(HALF, HALF)], out_block(d, half)[HALF:])
+        hidden_ref[:, columns] = (mixed_ref[:, columns] + mixed).astype(bf16)
 
     def term_step(f, _):
         term_ref[f] = dot_tn(rows_ref[...], hidden_ref[:, columns_of(f)]).reshape(
@@ -720,12 +726,10 @@
 
     core_copy.start()
     backward(1, (lambda: None, reduce_first))
-    add_grad_normed(0, QUERY, first=True)
     add_grad_normed(0, KEY)
+    add_grad_normed(0, VALUE)
     reduce_second()
-    add_grad_normed(0, VALUE)
     add_grad_normed(1, QUERY)
-    reduce_z()
 
     head_out = dot_nn(hidden_ref[...], w_head_shuffled[...])
     head_out = jnp.concatenate(
@@ -746,6 +750,8 @@
         for a in range(4):
             fine_ref[fine_rows(i, a), :] = shuffled_ref[cell_rows(i, a), :]
 
+    reduce_z()
+    add_grad_normed(1, KEY)
     for copy in z_copies:
         copy.wait_recv()
     summed = acc2[me]
@@ -754,7 +760,6 @@
     full_grad[core, outer, inner] = summed
     for copy in back:
         copy.start()
-    add_grad_normed(1, KEY)
     add_grad_normed(1, VALUE)
     for copy in back:
         copy.wait_recv()
@@ -815,6 +820,7 @@
         + [
             pltpu.VMEM((row_count, D), f32),
             pltpu.VMEM((row_count, 1), f32),
+            pltpu.VMEM((row_count, D), f32),
             pltpu.VMEM((row_count, D), bf16),
             pltpu.VMEM((GROUPS, row_count, HALF), bf16),
             pltpu.VMEM((GROUPS, key_count, HALF), bf16),

time: 100 us -> 101 us (1.010)
  no operation moved by 1% of the time
where the time goes in v5:
time: 101 us; the launch traced here: 100 us
  Pallas kernels  95.1 us (94%)
  local copies, waits for them, and re-layouts  4.62 us (5%)
    pallas_call x1, Pallas kernels, fused_shards(): pl.pallas_call(functools.partial(block_kernel, fsdp, lat_rows, lon_cols),...  95.1 us
    unnamed x5, local copies, waits for them, and re-layouts  4.62 us

profile of v5, /device:TPU:0, one launch (start us, length us, event | category | flops | bytes accessed | tf_op | source)
XLA Modules:
  0.0 100.4 jit_solution(6169914329343762337)
XLA Ops:
  0.6 95.1 %shard_map.94 = (f32[640,128]{1,0:T(8,128)}, bf16[256,1536]{1,0:T(8,128)(2,1)}, f32[2,2,2,40,384]{4,3,2,1,0:T(8,128)}) custom-call(bf16[256,1536]{1,0:T(8,128)(2,1)} %bitcast.15, f32[1536]{0:T(1024)} %gain_ref.1, bf16[2,2,2,48,2304]{4,3,2,1,0:T(8,128)(2,1)} %bitcast.14, bf16[2,2,48,1536]{3,2,1,0:T(8,128)(2,1)} %bitcast.16, bf16[320,384]{1,0:T(8,128)(2,1)} %bitcast.18, ...), custom_call_target="tpu_custom_call" | custom-call | flops 7000000000 | bytes 10000000 | tf_op jit(solution)/shard_map/pallas_call | solution.py:805
  95.7 0.0 copy-start
  95.7 1.8 %copy.13 = f32[1,20,32,128]{3,2,1,0:T(8,128)} copy(f32[1,20,32,128]{3,2,1,0:T(8,128)} %bitcast.13) | data formatting | bytes 655360
  97.5 2.1 %copy.14 = bf16[1,8,32,1536]{3,2,1,0:T(8,128)(2,1)} copy(bf16[1,8,32,1536]{3,2,1,0:T(8,128)(2,1)} %bitcast.11) | data formatting | bytes 1572864
  99.6 0.0 copy-done
  99.6 0.8 copy.15
Async XLA Ops:
  95.7 3.8 %copy-start = (f32[2,2,2,40,384]{4,3,2,1,0:T(8,128)S(1)}, f32[2,2,2,40,384]{4,3,2,1,0:T(8,128)}, u32[]{:S(2)}) copy-start(f32[2,2,2,40,384]{4,3,2,1,0:T(8,128)} %get-tuple-element.8) | copy-start | bytes 1474564
